TPU v7x, 256 devices: a whole 4x4x8 slice. The times are simulated.
256 devices in a mesh: fsdp: 32 (over z_lo, y, core), hst: 8 (over z_hi, x).
Axes of the slice: x: 4, y: 4, z: 8 (z_hi: 2, z_lo: 4; z = z_hi * 4 + z_lo), core: 2. Of those that a mesh axis runs over, the one named last changes fastest.
Arguments:
- tokens: bfloat16 [8192, 14848], P('fsdp'), may hold values from -6 to 6
- out_grad: bfloat16 [8192, 2048], P('fsdp', 'hst'), may hold values from -6 to 6
- param: float32 [14848, 2048], P('fsdp', 'hst'), may hold values from -0.125 to 0.125
- first: float32 [14848, 2048], P('fsdp', 'hst'), may hold values from -6 to 6
- second: float32 [14848, 2048], P('fsdp', 'hst'), may hold values from 0.25 to 4
- sources: int32 [8, 32, 8], P('hst'), may hold values from -1 to 511, as said below
Outputs:
- input_grad: bfloat16 [8192, 14848], P('fsdp', 'hst')
- new_state: float32 [3, 14848, 2048], P(None, 'fsdp', 'hst')
- backup_state: float32 [3, 14848, 2048], P(None, 'fsdp', 'hst')
- written: float32 [8, 32, 8, 29, 256], P('hst', 'fsdp')
Inputs may be any that keep to these rules, and one draw needn't show every extreme that they name: `sources`: an entry s >= 0 names piece s % 16 of owner s // 16 in the host's own group; -1 is an empty slot and empty slots come after filled ones. Within one host no piece is named twice. A writer names at most 2 pieces of one owner, and some writer of every host names exactly 2; some writer of every host fills all 8 slots.
All inputs are finite; a program needn't handle non-finite values.
Results may differ from a plain program's by a relative error of at most 0.015.
Values may be sent and summed in bfloat16 or wider, within the bound.
A program may use at most 128 MiB of HBM per device.

v0:
```python
import jax
import jax.numpy as jnp
from jax import lax
from jax.sharding import PartitionSpec as P

PIECES = 16
WCAP = 8
SCAP = 2


def from_behind(value, axis, steps):
    count = lax.axis_size(axis)
    pairs = [(source, (source + steps) % count) for source in range(count)]
    return lax.ppermute(value, axis, pairs)


def gelu_slope(pre):
    cdf = 0.5 * (1.0 + jax.scipy.special.erf(pre * 0.7071067811865476))
    pdf = jnp.exp(-0.5 * pre * pre) * 0.3989422804014327
    return cdf + pre * pdf


def adam_step(param, first, second, grad):
    moment = 0.8 * first + 0.2 * grad
    spread = 0.9 * second + 0.1 * grad * grad
    updated = param - 0.1 * (moment / (jnp.sqrt(spread) + 1e-08) + 0.1 * param)
    return (updated, moment, spread)


def on_device(tokens, out_grad, param, first, second, sources):
    tok_rows = tokens.shape[0]
    row_count = param.shape[0]
    col_count = param.shape[1]
    weight16 = param.astype(jnp.bfloat16)
    columns = tokens
    pre = jnp.dot(
        columns,
        lax.all_gather(weight16, "fsdp", axis=0, tiled=True),
        preferred_element_type=jnp.float32,
    )
    dz = (out_grad.astype(jnp.float32) * gelu_slope(pre)).astype(jnp.bfloat16)
    dims_back = (((1,), (1,)), ((), ()))
    partial_in = lax.dot_general(
        dz,
        lax.all_gather(weight16, "fsdp", axis=0, tiled=True),
        dims_back,
        preferred_element_type=jnp.float32,
    )
    columns = tokens
    grad_sum = lax.psum_scatter(
        lax.dot_general(
            columns, dz, (((0,), (0,)), ((), ())), preferred_element_type=jnp.float32
        ).astype(jnp.bfloat16),
        "fsdp",
        scatter_dimension=0,
        tiled=True,
    ).astype(jnp.float32)
    input_grad = lax.psum_scatter(
        partial_in.astype(jnp.bfloat16), "hst", scatter_dimension=1, tiled=True
    )
    grad = grad_sum / jnp.sqrt(jnp.float32(tok_rows * lax.axis_size("fsdp")))
    updated, moment, spread = adam_step(param, first, second, grad)
    new_state = jnp.stack([updated, moment, spread])
    backup_state = from_behind(new_state.astype(jnp.bfloat16), "hst", 1).astype(new_state.dtype)
    me = lax.axis_index("fsdp")
    fsdp_count = lax.axis_size("fsdp")
    table = sources[0]
    rows_piece = row_count // PIECES
    owners = table // PIECES
    mine = (owners == me) & (table >= 0)
    rank = jnp.cumsum(mine.astype(jnp.int32), axis=1) - 1
    slot_pick = mine[:, None, :] & (
        rank[:, None, :] == jnp.arange(SCAP, dtype=jnp.int32)[None, :, None]
    )
    piece_of = table % PIECES
    piece_match = (
        piece_of[:, None, :, None] == jnp.arange(PIECES, dtype=jnp.int32)[None, None, None, :]
    )
    selector = jnp.sum((slot_pick[..., None] & piece_match).astype(jnp.float32), axis=2)
    flat_pieces = updated.reshape(PIECES, rows_piece * col_count)
    outgoing = jnp.einsum("dkp,pq->dkq", selector, flat_pieces, precision=lax.Precision.HIGHEST)
    arrived = lax.all_to_all(
        outgoing.astype(jnp.bfloat16), "fsdp", split_axis=0, concat_axis=0, tiled=True
    ).astype(outgoing.dtype)
    own_row = lax.dynamic_index_in_dim(table, me, 0, keepdims=False)
    own_owner = own_row // PIECES
    valid = own_row >= 0
    slot_ids = jnp.arange(WCAP, dtype=jnp.int32)
    earlier = (slot_ids[None, :] < slot_ids[:, None]) & (own_owner[None, :] == own_owner[:, None])
    own_rank = jnp.sum(earlier.astype(jnp.int32), axis=1)
    index = jnp.maximum(own_owner, 0) * SCAP + own_rank
    picked = jnp.take(arrived.reshape(fsdp_count * SCAP, rows_piece * col_count), index, axis=0)
    picked = jnp.where(valid[:, None], picked, jnp.float32(0.0))
    written = picked.reshape(1, 1, WCAP, rows_piece, col_count)
    return (input_grad, new_state, backup_state, written)


def solution(mesh):
    return jax.shard_map(
        on_device,
        mesh=mesh,
        in_specs=(
            P("fsdp", None),
            P("fsdp", "hst"),
            P("fsdp", "hst"),
            P("fsdp", "hst"),
            P("fsdp", "hst"),
            P("hst", None, None),
        ),
        out_specs=(
            P("fsdp", "hst"),
            P(None, "fsdp", "hst"),
            P(None, "fsdp", "hst"),
            P("hst", "fsdp", None, None, None),
        ),
        check_vma=False,
    )
```

profile of v0, /device:TPU:1, one launch (start us, length us, event | category | flops | bytes accessed | tf_op | source)
XLA Modules:
  0.0 475.8 jit_solution(9085632774163887810)
XLA Ops:
  7.2 0.0 all-gather.2.cloned.1.call-start
  7.2 1.7 convert_element_type.45
  9.0 0.0 all-gather.2.cloned.1.call-update
  9.0 0.0 copy-start.1
  9.0 0.0 reduce-scatter.7.cloned.1.call-start
  9.0 73.9 %all-gather.2.cloned.1.call-done = bf16[14848,256]{1,0:T(8,128)(2,1)} async-done(((bf16[464,256]{1,0:T(8,128)(2,1)}), bf16[14848,256]{1,0:T(8,128)(2,1)}) %all-gather.2.cloned.1.call-update) | async-done | bytes 7602192 | tf_op jit(solution)/shard_map/all_gather | solution.py:38
  82.9 7.4 %fusion.47 = f32[256,256]{1,0:T(8,128)S(1)} fusion(bf16[256,14848]{1,0:T(8,128)(2,1)} %param.6, bf16[14848,256]{1,0:T(8,128)(2,1)} %all-gather.2.cloned.1.call-done), kind=kOutput, calls=%fused_computation.85 | convolution fusion | flops 1946157056 | bytes 15466496 | tf_op jit(solution)/shard_map/dot_general | solution.py:36
  90.4 0.0 copy-done.1
  90.4 8.5 %fusion = bf16[14848,256]{0,1:T(8,128)(2,1)} fusion(bf16[256,14848]{1,0:T(8,128)(2,1)} %param.6, f32[256,256]{1,0:T(8,128)S(1)} %fusion.47, bf16[256,256]{1,0:T(8,128)(2,1)S(1)} %copy-done.1), kind=kOutput, calls=%fused_computation.3 | convolution fusion | flops 1950679040 | bytes 15597568 | tf_op jit(solution)/shard_map/dot_general | solution.py:51
  98.9 10.5 %copy.51 = bf16[14848,256]{1,0:T(8,128)(2,1)} copy(bf16[14848,256]{0,1:T(8,128)(2,1)} %fusion) | data formatting | bytes 15204352
  109.4 0.0 reduce-scatter.7.cloned.1.call-update
  109.4 0.0 reduce-scatter.5.cloned.1.call-start
  109.5 8.5 %convolution_convert_fusion.1 = bf16[256,14848]{0,1:T(8,128)(2,1)} fusion(bf16[14848,256]{1,0:T(8,128)(2,1)} %all-gather.2.cloned.1.call-done, f32[256,256]{1,0:T(8,128)S(1)} %fusion.47, bf16[256,256]{1,0:T(8,128)(2,1)S(1)} %copy-done.1), kind=kOutput, calls=%fused_computation.2 | convolution fusion | flops 1950679040 | bytes 15597568 | tf_op jit(solution)/shard_map/dot_general | solution.py:43
  117.9 0.0 copy-start.4
  117.9 0.0 copy-start
  117.9 0.0 copy-start.2
  117.9 0.0 copy-start.3
  117.9 0.0 reduce-scatter.5.cloned.1.call-update
  118.0 0.6 copy-done.4
  118.7 140.2 %reduce-scatter.7.cloned.1.call-done = bf16[464,256]{1,0:T(8,128)(2,1)} async-done(((bf16[14848,256]{1,0:T(8,128)(2,1)}), bf16[464,256]{1,0:T(8,128)(2,1)}) %reduce-scatter.7.cloned.1.call-update) | async-done | bytes 237584 | tf_op jit(solution)/shard_map/reduce_scatter | solution.py:50
  258.9 0.0 copy-done
  258.9 0.0 copy-done.2
  258.9 0.0 copy-done.3
  258.9 1.3 multiply_subtract_fusion
  260.2 0.1 reshape.305
  260.4 1.7 convolution_convert_fusion.2
  262.1 1.9 copy.50
  264.0 9.6 %all-to-all-start = ((bf16[32,2,7424]{2,1,0:T(2,128)(2,1)}), bf16[32,2,7424]{2,1,0:T(2,128)(2,1)S(1)}, u32[]{:S(2)}, u32[]{:S(2)}) async-start(bf16[32,2,7424]{2,1,0:T(2,128)(2,1)} %copy.50), calls=%async_computation.1 | async-start | bytes 1900544 | tf_op jit(solution)/shard_map/all_to_all | solution.py:82
  273.7 0.2 dynamic-slice_reduce_fusion
  273.8 1.2 fusion.46
  275.1 1.6 collective-permute-start
  276.7 0.2 convert_reduce_fusion.1
  276.9 80.1 %collective-permute-done = bf16[3,464,256]{2,1,0:T(8,128)(2,1)S(1)} collective-permute-done((bf16[3,464,256]{2,1,0:T(8,128)(2,1)S(1)}, bf16[3,464,256]{2,1,0:T(8,128)(2,1)S(1)}, u32[]{:S(2)}, u32[]{:S(2)}) %collective-permute-start) | collective-permute-done | bytes 712736 | tf_op jit(solution)/shard_map/ppermute | solution.py:14
  357.0 1.2 convert_element_type.52
  358.2 0.0 all-to-all-done
  358.2 0.3 reshape.296
  358.5 0.6 gather_fusion
  359.1 0.8 select_select_fusion
  359.9 109.4 %reduce-scatter.5.cloned.1.call-done = bf16[256,1856]{0,1:T(8,128)(2,1)} async-done(((bf16[256,14848]{0,1:T(8,128)(2,1)}), bf16[256,1856]{0,1:T(8,128)(2,1)}) %reduce-scatter.5.cloned.1.call-update) | async-done | bytes 950288 | tf_op jit(solution)/shard_map/reduce_scatter | solution.py:58
  (11 shorter events, 0.2 us)
Async XLA Ops:
  7.2 75.7 %all-gather.2.cloned.1.call-start = ((), (), s32[]{:S(2)}) async-start(), calls=%async_computation.3 | async-start | bytes 7839744 | tf_op jit(solution)/shard_map/all_gather | solution.py:38
  9.0 81.4 %copy-start.1 = (bf16[256,256]{1,0:T(8,128)(2,1)S(1)}, bf16[256,256]{1,0:T(8,128)(2,1)}, u32[]{:S(2)}) copy-start(bf16[256,256]{1,0:T(8,128)(2,1)} %param.7) | copy-start | bytes 393220
  9.0 249.9 %reduce-scatter.7.cloned.1.call-start = ((), (), s32[]{:S(2)}) async-start(), calls=%async_computation.5 | async-start | bytes 7839744 | tf_op jit(solution)/shard_map/reduce_scatter | solution.py:50
  109.4 359.9 %reduce-scatter.5.cloned.1.call-start = ((), (), s32[]{:S(2)}) async-start(), calls=%async_computation.4 | async-start | bytes 8552448 | tf_op jit(solution)/shard_map/reduce_scatter | solution.py:58
  117.9 0.7 copy-start.4
  117.9 141.0 %copy-start = (f32[464,256]{1,0:T(8,128)S(1)}, f32[464,256]{1,0:T(8,128)}, u32[]{:S(2)}) copy-start(f32[464,256]{1,0:T(8,128)} %param.8) | copy-start | bytes 1425412
  117.9 141.0 %copy-start.2 = (f32[464,256]{1,0:T(8,128)S(1)}, f32[464,256]{1,0:T(8,128)}, u32[]{:S(2)}) copy-start(f32[464,256]{1,0:T(8,128)} %param.9) | copy-start | bytes 1425412
  117.9 141.0 %copy-start.3 = (f32[464,256]{1,0:T(8,128)S(1)}, f32[464,256]{1,0:T(8,128)}, u32[]{:S(2)}) copy-start(f32[464,256]{1,0:T(8,128)} %param.10) | copy-start | bytes 1425412
  264.0 94.2 %all-to-all-start = ((bf16[32,2,7424]{2,1,0:T(2,128)(2,1)}), bf16[32,2,7424]{2,1,0:T(2,128)(2,1)S(1)}, u32[]{:S(2)}, u32[]{:S(2)}) async-start(bf16[32,2,7424]{2,1,0:T(2,128)(2,1)} %copy.50), calls=%async_computation.1 | async-start | bytes 1900544 | tf_op jit(solution)/shard_map/all_to_all | solution.py:82
  275.1 81.9 %collective-permute-start = (bf16[3,464,256]{2,1,0:T(8,128)(2,1)S(1)}, bf16[3,464,256]{2,1,0:T(8,128)(2,1)S(1)}, u32[]{:S(2)}, u32[]{:S(2)}) collective-permute-start(bf16[3,464,256]{2,1,0:T(8,128)(2,1)S(1)} %get-tuple-element.22), channel_id=1, source_target_pairs={{0,1},{1,2},{2,3},{3,4},{4,5},{5,6},{6,7},{7,0},{8,9},{9,10},{10,1... | collective-permute-start | bytes 2138120 | tf_op jit(solution)/shard_map/ppermute | solution.py:14
Sparse Core Ops, SparseCore 0:
  10.4 72.4 all-gather.1
  109.5 149.3 reduce-scatter.6
  264.3 204.9 reduce-scatter.4
where the time goes:
time: 476 us
  waiting for transfers between devices  404 us (85%)
  matrix products  26.1 us (5%)
  local copies, waits for them, and re-layouts  14.4 us (3%)
  between operations  13.9 us (3%)
  starting transfers between devices  11.3 us (2%)
  other arithmetic  6.63 us (1%)
    reduce_scatter x1, waiting for transfers between devices, on_device(): lax.psum_scatter(lax.dot_general(columns, dz, (((0,), (0,)), ((), ())), p...  140 us
    reduce_scatter x1, waiting for transfers between devices, on_device(): lax.psum_scatter(partial_in.astype(jnp.bfloat16), 'hst', scatter_dimensio...  109 us
    ppermute x1, waiting for transfers between devices, from_behind(): return lax.ppermute(value, axis, pairs)  80.1 us
    all_gather x1, waiting for transfers between devices, on_device(): lax.all_gather(weight16, 'fsdp', axis=0, tiled=True)  73.9 us
    unnamed x11, local copies, waits for them, and re-layouts  11.2 us
    all_to_all x1, starting transfers between devices, on_device(): lax.all_to_all(outgoing.astype(jnp.bfloat16), 'fsdp', split_axis=0, conca...  9.64 us
  transfers between devices with their start and end apart: 5, of which 4 were waited for; matrix products, arithmetic and copies ran while one was open for 4% of the time, Pallas kernels for 0%

commit v1 on v0

--- a/solution.py
+++ b/solution.py
@@ -1,21 +1,27 @@
+import functools
+
 import jax
 import jax.numpy as jnp
 from jax import lax
+from jax.experimental import pallas as pl
+from jax.experimental.pallas import tpu as pltpu
 from jax.sharding import PartitionSpec as P
 
 PIECES = 16
 WCAP = 8
 SCAP = 2
-
-
-def from_behind(value, axis, steps):
-    count = lax.axis_size(axis)
-    pairs = [(source, (source + steps) % count) for source in range(count)]
-    return lax.ppermute(value, axis, pairs)
+MESH = pl.DeviceIdType.MESH
+BF16 = jnp.bfloat16
+F32 = jnp.float32
+NZ, NY = 4, 4
+TOK = 256
+RB = 464
+CB = 256
+HA = 240
 
 
 def gelu_slope(pre):
-    cdf = 0.5 * (1.0 + jax.scipy.special.erf(pre * 0.7071067811865476))
+    cdf = 0.5 * (1.0 + lax.erf(pre * 0.7071067811865476))
     pdf = jnp.exp(-0.5 * pre * pre) * 0.3989422804014327
     return cdf + pre * pdf
 
@@ -27,41 +33,250 @@
     return (updated, moment, spread)
 
 
+def rows_of(f):
+    return pl.ds(pl.multiple_of(f * RB, 16), RB)
+
+
+def core_kernel(
+    tokens, out_grad, param, grad_out, dz_out,
+    tok, tokT, w, part, rxp, chip, sendh, rxh, sendf, rxf, sendz, rxz,
+    tok_sem, ag_s, ag_r, rs_s, rs_r,
+):
+    f = lax.axis_index("fsdp")
+    z, y, c = f // 8, (f // 2) % 4, f % 2
+    yr, yl, yo = (y + 1) % 4, (y + 3) % 4, (y + 2) % 4
+    zk = [z, z + 1 - 2 * (z % 2), (z + 2) % 4, 3 - z]
+
+    def at(zz, yy, cc):
+        return {"fsdp": zz * 8 + yy * 2 + cc}
+
+    def idx(zz, yy, cc):
+        return zz * 8 + yy * 2 + cc
+
+    right, left, partner = at(z, yr, c), at(z, yl, c), at(z, y, 1 - c)
+
+    tok_copy = pltpu.make_async_copy(tokens, tok, tok_sem)
+    tok_copy.start()
+    w[rows_of(f), :] = param[...].astype(BF16)
+
+    barrier = pltpu.get_barrier_semaphore()
+    for peer in (right, left, partner, at(zk[1], y, c), at(zk[2], y, c), at(zk[3], y, c)):
+        pl.semaphore_signal(barrier, inc=1, device_id=peer, device_id_type=MESH)
+    pl.semaphore_wait(barrier, 6)
+
+    pending = []
+
+    def send(src, dst, s_sem, r_sem, to):
+        copy = pltpu.make_async_remote_copy(
+            src_ref=src, dst_ref=dst, send_sem=s_sem, recv_sem=r_sem, device_id=to, device_id_type=MESH
+        )
+        copy.start()
+        pending.append(copy)
+        return copy
+
+    def ag_send(block, lo, n, k, j, to):
+        ref = w.at[pl.ds(pl.multiple_of(block * RB + lo, 16), n), :]
+        return send(ref, ref, ag_s.at[k * 8 + j], ag_r.at[k * 8 + j], to)
+
+    zsend = {}
+    own = [None] * 4
+    core = {}
+
+    def issue(k):
+        b = idx(zk[k], y, c)
+        own[k] = (ag_send(b, 0, RB, k, 0, right), ag_send(b, 0, RB, k, 1, left))
+        core[k, 0] = ag_send(b, 0, RB, k, 4, partner)
+
+    issue(0)
+    for k in (1, 2, 3):
+        ref = w.at[rows_of(f), :]
+        zsend[k] = send(ref, ref, ag_s.at[32 + k], ag_r.at[32 + k], at(zk[k], y, c))
+
+    tok_copy.wait()
+
+    def transpose_some(lo, hi):
+        def step(i, carry):
+            cols = pl.ds(pl.multiple_of(i * 512, 512), 512)
+            tokT[cols, :] = tok[:, cols].T
+            return carry
+
+        lax.fori_loop(lo, hi, step, 0)
+
+    halves = {}
+
+    def forward(k):
+        own[k][0].wait_recv()
+        b = idx(zk[k], yl, c)
+        ha = ag_send(b, 0, HA, k, 2, right)
+        core[k, 1] = ag_send(b, 0, RB, k, 5, partner)
+        own[k][1].wait_recv()
+        b = idx(zk[k], yr, c)
+        hb = ag_send(b, HA, RB - HA, k, 3, left)
+        core[k, 2] = ag_send(b, 0, RB, k, 6, partner)
+        halves[k] = (ha, hb)
+
+    def last(k):
+        halves[k][0].wait_recv()
+        halves[k][1].wait_recv()
+        core[k, 3] = ag_send(idx(zk[k], yo, c), 0, RB, k, 7, partner)
+
+    transpose_some(0, 8)
+    zsend[1].wait_recv()
+    issue(1)
+    forward(0)
+    transpose_some(8, 15)
+    zsend[2].wait_recv()
+    issue(2)
+    last(0)
+    forward(1)
+    transpose_some(15, 22)
+    zsend[3].wait_recv()
+    issue(3)
+    last(1)
+    forward(2)
+    transpose_some(22, 29)
+    last(2)
+    forward(3)
+    last(3)
+    for k in range(4):
+        for j in range(4):
+            core[k, j].wait_recv()
+
+    def pre_step(i, acc):
+        cols = pl.ds(pl.multiple_of(i * 3712, 128), 3712)
+        return acc + jnp.dot(tok[:, cols], w[cols, :], preferred_element_type=F32)
+
+    pre = lax.fori_loop(0, 4, pre_step, jnp.zeros((TOK, CB), F32))
+    dz = (out_grad[...].astype(F32) * gelu_slope(pre)).astype(BF16)
+    dz_out[...] = dz
+
+    swap = []
+    for s, k in enumerate((3, 2, 1, 0)):
+        def partner_block(j, carry, k=k, s=s):
+            part[s, j] = jnp.dot(
+                tokT[rows_of(idx(zk[k], j, 1 - c)), :], dz_out[...], preferred_element_type=F32
+            ).astype(BF16)
+            return carry
+
+        lax.fori_loop(0, 4, partner_block, 0)
+        swap.append(send(part.at[s], rxp.at[s], rs_s.at[s], rs_r.at[s], partner))
+
+    def chip_block(k, s, yy):
+        mine = jnp.dot(tokT[rows_of(idx(zk[k], yy, c)), :], dz_out[...], preferred_element_type=F32)
+        return mine + rxp[s, yy].astype(F32)
+
+    hsend = []
+    for s, k in enumerate((3, 2, 1, 0)):
+        swap[s].wait_recv()
+        sendh[s] = chip_block(k, s, yo).astype(BF16)
+        a = send(sendh.at[s, pl.ds(0, HA)], rxh.at[s, pl.ds(0, HA)], rs_s.at[4 + s], rs_r.at[4 + s], right)
+        b = send(
+            sendh.at[s, pl.ds(HA, RB - HA)], rxh.at[s, pl.ds(HA, RB - HA)], rs_s.at[8 + s], rs_r.at[8 + s], left
+        )
+        hsend.append((a, b))
+        chip[s, 0] = chip_block(k, s, yr)
+        chip[s, 1] = chip_block(k, s, yl)
+        chip[s, 2] = chip_block(k, s, y)
+
+    fsend = []
+    zout = []
+
+    def full(s):
+        hsend[s][0].wait_recv()
+        sendf[s, 0, pl.ds(0, HA)] = (chip[s, 0, pl.ds(0, HA)] + rxh[s, pl.ds(0, HA)].astype(F32)).astype(BF16)
+        sendf[s, 0, pl.ds(HA, RB - HA)] = chip[s, 0, pl.ds(HA, RB - HA)].astype(BF16)
+        a = send(sendf.at[s, 0], rxf.at[s, 0], rs_s.at[12 + s], rs_r.at[12 + s], right)
+        hsend[s][1].wait_recv()
+        sendf[s, 1, pl.ds(0, HA)] = chip[s, 1, pl.ds(0, HA)].astype(BF16)
+        sendf[s, 1, pl.ds(HA, RB - HA)] = (
+            chip[s, 1, pl.ds(HA, RB - HA)] + rxh[s, pl.ds(HA, RB - HA)].astype(F32)
+        ).astype(BF16)
+        b = send(sendf.at[s, 1], rxf.at[s, 1], rs_s.at[16 + s], rs_r.at[16 + s], left)
+        fsend.append((a, b))
+
+    def ring_sum(s):
+        fsend[s][0].wait_recv()
+        fsend[s][1].wait_recv()
+        return chip[s, 2] + rxf[s, 0].astype(F32) + rxf[s, 1].astype(F32)
+
+    def line(s, k):
+        sendz[s] = ring_sum(s).astype(BF16)
+        zout.append(send(sendz.at[s], rxz.at[s], rs_s.at[20 + s], rs_r.at[20 + s], at(zk[k], y, c)))
+
+    full(0)
+    full(1)
+    line(0, 3)
+    full(2)
+    line(1, 2)
+    full(3)
+    line(2, 1)
+    total = ring_sum(3)
+    for s in range(3):
+        zout[s].wait_recv()
+        total = total + rxz[s].astype(F32)
+    grad_out[...] = total * (1.0 / 90.50966799187809)
+    for copy in pending:
+        copy.wait_send()
+
+
+def core_call(tokens, out_grad, param):
+    vmem = pl.BlockSpec(memory_space=pltpu.VMEM)
+    return pl.pallas_call(
+        core_kernel,
+        name="slab",
+        out_shape=(jax.ShapeDtypeStruct((RB, CB), F32), jax.ShapeDtypeStruct((TOK, CB), BF16)),
+        in_specs=[pl.BlockSpec(memory_space=pl.ANY), vmem, vmem],
+        out_specs=(vmem, vmem),
+        scratch_shapes=[
+            pltpu.VMEM((TOK, 32 * RB), BF16),
+            pltpu.VMEM((32 * RB, TOK), BF16),
+            pltpu.VMEM((32 * RB, CB), BF16),
+            pltpu.VMEM((4, 4, RB, CB), BF16),
+            pltpu.VMEM((4, 4, RB, CB), BF16),
+            pltpu.VMEM((4, 3, RB, CB), F32),
+            pltpu.VMEM((4, RB, CB), BF16),
+            pltpu.VMEM((4, RB, CB), BF16),
+            pltpu.VMEM((4, 2, RB, CB), BF16),
+            pltpu.VMEM((4, 2, RB, CB), BF16),
+            pltpu.VMEM((3, RB, CB), BF16),
+            pltpu.VMEM((3, RB, CB), BF16),
+            pltpu.SemaphoreType.DMA,
+            pltpu.SemaphoreType.DMA((36,)),
+            pltpu.SemaphoreType.DMA((36,)),
+            pltpu.SemaphoreType.DMA((24,)),
+            pltpu.SemaphoreType.DMA((24,)),
+        ],
+        compiler_params=pltpu.CompilerParams(
+            collective_id=0, has_side_effects=True, vmem_limit_bytes=60 * 1024 * 1024
+        ),
+        cost_estimate=pl.CostEstimate(flops=4 * TOK * 32 * RB * CB, bytes_accessed=300_000_000, transcendentals=TOK * CB),
+    )(tokens, out_grad, param)
+
+
+def from_behind(value, axis, steps):
+    count = lax.axis_size(axis)
+    pairs = [(source, (source + steps) % count) for source in range(count)]
+    return lax.ppermute(value, axis, pairs)
+
+
 def on_device(tokens, out_grad, param, first, second, sources):
-    tok_rows = tokens.shape[0]
     row_count = param.shape[0]
     col_count = param.shape[1]
-    weight16 = param.astype(jnp.bfloat16)
-    columns = tokens
-    pre = jnp.dot(
-        columns,
-        lax.all_gather(weight16, "fsdp", axis=0, tiled=True),
-        preferred_element_type=jnp.float32,
-    )
-    dz = (out_grad.astype(jnp.float32) * gelu_slope(pre)).astype(jnp.bfloat16)
-    dims_back = (((1,), (1,)), ((), ()))
-    partial_in = lax.dot_general(
-        dz,
-        lax.all_gather(weight16, "fsdp", axis=0, tiled=True),
-        dims_back,
-        preferred_element_type=jnp.float32,
-    )
-    columns = tokens
-    grad_sum = lax.psum_scatter(
-        lax.dot_general(
-            columns, dz, (((0,), (0,)), ((), ())), preferred_element_type=jnp.float32
-        ).astype(jnp.bfloat16),
-        "fsdp",
-        scatter_dimension=0,
-        tiled=True,
-    ).astype(jnp.float32)
-    input_grad = lax.psum_scatter(
-        partial_in.astype(jnp.bfloat16), "hst", scatter_dimension=1, tiled=True
-    )
-    grad = grad_sum / jnp.sqrt(jnp.float32(tok_rows * lax.axis_size("fsdp")))
+    weight16 = param.astype(BF16)
+    pairs = [(f * 8 + h, (4 * h + f % 4) * 8 + f // 4) for f in range(32) for h in range(8)]
+    w2 = lax.all_gather(lax.ppermute(weight16, ("fsdp", "hst"), pairs), "fsdp", axis=0)
+    grad, dz = core_call(tokens, out_grad, param)
+    dz_all = lax.all_gather(dz, "hst", axis=0)
+    w2 = w2.reshape(8, 4 * RB, CB)
+    input_grad = lax.dot_general(
+        dz_all.transpose(1, 0, 2).reshape(TOK, 8 * CB),
+        w2.transpose(1, 0, 2).reshape(4 * RB, 8 * CB),
+        (((1,), (1,)), ((), ())),
+        preferred_element_type=F32,
+    ).astype(BF16)
     updated, moment, spread = adam_step(param, first, second, grad)
     new_state = jnp.stack([updated, moment, spread])
-    backup_state = from_behind(new_state.astype(jnp.bfloat16), "hst", 1).astype(new_state.dtype)
+    backup_state = from_behind(new_state.astype(BF16), "hst", 1).astype(new_state.dtype)
     me = lax.axis_index("fsdp")
     fsdp_count = lax.axis_size("fsdp")
     table = sources[0]

time: 476 us -> 266 us (0.56)
  waiting for transfers between devices: 404 us -> 110 us
  Pallas kernels: 0 us -> 94.6 us
  matrix products: 26.1 us -> 8.27 us
  starting transfers between devices: 11.3 us -> 29 us
  local copies, waits for them, and re-layouts: 14.4 us -> 3.87 us
    reduce_scatter x2 -> x0, waiting for transfers between devices: 250 us -> none  [the longest x1 140 us: on_device(): lax.psum_scatter(lax.dot_general(columns, dz, (((0,), (0,)), ((), ())), p...]
    pallas_call x0 -> x1, Pallas kernels: none -> 94.6 us  [core_call(): pl.pallas_call(core_kernel, name='slab', out_shape=(jax.ShapeDtypeStruct(...]
    all_gather x1 -> x2, waiting for transfers between devices: 73.9 us -> 47.1 us  [the longest x1 47.1 us: on_device(): lax.all_gather(lax.ppermute(weight16, ('fsdp', 'hst'), pairs), 'fsdp', ax...]
    all_to_all x1, starting transfers between devices: 9.64 us -> 28.3 us  [on_device(): lax.all_to_all(outgoing.astype(jnp.bfloat16), 'fsdp', split_axis=0, conca...]
    dot_general x3 -> x1, matrix products: 24.4 us -> 6.6 us  [on_device(): lax.dot_general(dz_all.transpose(1, 0, 2).reshape(TOK, 8 * CB), w2.transp...]
    ppermute x1, waiting for transfers between devices: 80.1 us -> 63.2 us  [from_behind(): return lax.ppermute(value, axis, pairs)]
    unnamed x11 -> x10, local copies, waits for them, and re-layouts: 11.2 us -> 0.73 us
  transfers between devices with their start and end apart: 5 -> 5, of which waited for: 4 -> 2; matrix products, arithmetic and copies ran while one was open for 4% -> 4% of each run, Pallas kernels for 0% -> 0%
where the time goes in v1:
time: 266 us
  waiting for transfers between devices  110 us (41%)
  Pallas kernels  94.6 us (36%)
  starting transfers between devices  29 us (11%)
  between operations  14.2 us (5%)
  matrix products  8.27 us (3%)
  other arithmetic  5.19 us (2%)
  local copies, waits for them, and re-layouts  3.87 us (1%)
    pallas_call x1, Pallas kernels, core_call(): pl.pallas_call(core_kernel, name='slab', out_shape=(jax.ShapeDtypeStruct(...  94.6 us
    ppermute x1, waiting for transfers between devices, from_behind(): return lax.ppermute(value, axis, pairs)  63.2 us
    all_gather x1, waiting for transfers between devices, on_device(): lax.all_gather(lax.ppermute(weight16, ('fsdp', 'hst'), pairs), 'fsdp', ax...  47.1 us
    all_to_all x1, starting transfers between devices, on_device(): lax.all_to_all(outgoing.astype(jnp.bfloat16), 'fsdp', split_axis=0, conca...  28.3 us
    dot_general x1, matrix products, on_device(): lax.dot_general(dz_all.transpose(1, 0, 2).reshape(TOK, 8 * CB), w2.transp...  6.6 us
  transfers between devices with their start and end apart: 5, of which 2 were waited for; matrix products, arithmetic and copies ran while one was open for 4% of the time, Pallas kernels for 0%

profile of v1, /device:TPU:1, one launch (start us, length us, event | category | flops | bytes accessed | tf_op | source)
XLA Modules:
  0.0 265.5 jit_solution(4378307167323273060)
XLA Ops:
  7.2 0.0 copy-start
  7.2 0.0 copy-start.1
  7.2 0.0 copy-start.2
  7.2 0.0 all-gather.5.cloned.1.call-start
  7.2 94.6 %slab.1 = (f32[464,256]{1,0:T(8,128)}, bf16[256,256]{1,0:T(8,128)(2,1)}) custom-call(bf16[256,14848]{1,0:T(8,128)(2,1)} %tokens.1, bf16[256,256]{1,0:T(8,128)(2,1)} %out_grad.1, f32[464,256]{1,0:T(8,128)} %param.13), custom_call_target="tpu_custom_call" | custom-call | flops 3892314112 | bytes 300000000 | tf_op jit(solution)/shard_map/slab/pallas_call | solution.py:224
  101.9 0.0 all-gather.5.cloned.1.call-update
  101.9 0.0 all-gather.7.cloned.1.call-start
  101.9 0.0 copy-done
  101.9 0.0 copy-done.1
  102.0 0.0 copy-done.2
  102.0 0.0 copy-start.4
  102.0 1.4 multiply_subtract_fusion
  103.4 0.7 collective-permute-start
  104.0 0.0 collective-permute-done
  104.0 0.0 copy-start.3
  104.1 0.7 copy-done.3
  104.8 0.0 all-gather.7.cloned.1.call-update
  104.8 0.1 reshape.315
  105.0 0.0 copy-done.4
  105.1 1.7 convolution_convert_fusion
  106.8 1.9 copy.21
  108.7 28.3 %all-to-all-start = ((bf16[32,2,7424]{2,1,0:T(2,128)(2,1)}), bf16[32,2,7424]{2,1,0:T(2,128)(2,1)S(1)}, u32[]{:S(2)}, u32[]{:S(2)}) async-start(bf16[32,2,7424]{2,1,0:T(2,128)(2,1)} %copy.21), calls=%async_computation | async-start | bytes 1900544 | tf_op jit(solution)/shard_map/all_to_all | solution.py:297
  137.0 1.5 fusion.14
  138.4 0.0 collective-permute-start.1
  138.4 0.2 dynamic-slice_reduce_fusion
  138.6 0.2 convert_reduce_fusion.1
  138.9 63.2 %collective-permute-done.1 = bf16[3,464,256]{2,1,0:T(8,128)(2,1)S(1)} collective-permute-done((bf16[3,464,256]{2,1,0:T(8,128)(2,1)}, bf16[3,464,256]{2,1,0:T(8,128)(2,1)S(1)}, u32[]{:S(2)}, u32[]{:S(2)}) %collective-permute-start.1) | collective-permute-done | bytes 712736 | tf_op jit(solution)/shard_map/ppermute | solution.py:259
  202.1 1.2 convert_element_type.32
  203.3 0.0 all-to-all-done
  203.3 0.3 reshape.302
  203.6 0.6 gather_fusion
  204.2 0.8 select_select_fusion
  205.0 0.0 all-gather.5.cloned.1.call-done
  205.0 47.1 %all-gather.7.cloned.1.call-done = bf16[14848,256]{1,0:T(8,128)(2,1)} async-done(((bf16[464,256]{1,0:T(8,128)(2,1)}), bf16[14848,256]{1,0:T(8,128)(2,1)}) %all-gather.7.cloned.1.call-update) | async-done | bytes 7602192 | tf_op jit(solution)/shard_map/all_gather | solution.py:267
  252.1 6.6 %fusion = bf16[256,1856]{0,1:T(8,128)(2,1)} fusion(bf16[256,8,256]{2,0,1:T(8,128)(2,1)} %bitcast.71, bf16[1856,8,256]{2,0,1:T(8,128)(2,1)} %bitcast.70), kind=kOutput, calls=%fused_computation.3 | convolution fusion | flops 1946632192 | bytes 9601024 | tf_op jit(solution)/shard_map/dot_general | solution.py:271
  (11 shorter events, 0.2 us)
Async XLA Ops:
  7.2 94.8 %copy-start = (f32[464,256]{1,0:T(8,128)S(1)}, f32[464,256]{1,0:T(8,128)}, u32[]{:S(2)}) copy-start(f32[464,256]{1,0:T(8,128)} %param.13) | copy-start | bytes 1425412
  7.2 94.8 %copy-start.1 = (f32[464,256]{1,0:T(8,128)S(1)}, f32[464,256]{1,0:T(8,128)}, u32[]{:S(2)}) copy-start(f32[464,256]{1,0:T(8,128)} %param.10) | copy-start | bytes 1425412
  7.2 94.8 %copy-start.2 = (f32[464,256]{1,0:T(8,128)S(1)}, f32[464,256]{1,0:T(8,128)}, u32[]{:S(2)}) copy-start(f32[464,256]{1,0:T(8,128)} %param.11) | copy-start | bytes 1425412
  7.2 197.8 %all-gather.5.cloned.1.call-start = ((), (), s32[]{:S(2)}) async-start(), calls=%async_computation.1 | async-start | bytes 1179648 | tf_op jit(solution)/shard_map/all_gather | solution.py:269
  101.9 150.2 %all-gather.7.cloned.1.call-start = ((), (), s32[]{:S(2)}) async-start(), calls=%async_computation.2 | async-start | bytes 7839744 | tf_op jit(solution)/shard_map/all_gather | solution.py:267
  102.0 3.0 %copy-start.4 = (s32[1,32,8]{1,2,0:T(8,128)S(1)}, s32[1,32,8]{1,2,0:T(8,128)}, u32[]{:S(2)}) copy-start(s32[1,32,8]{1,2,0:T(8,128)} %param.12) | copy-start | bytes 3076
  103.4 0.7 collective-permute-start
  104.0 0.7 copy-start.3
  108.7 94.6 %all-to-all-start = ((bf16[32,2,7424]{2,1,0:T(2,128)(2,1)}), bf16[32,2,7424]{2,1,0:T(2,128)(2,1)S(1)}, u32[]{:S(2)}, u32[]{:S(2)}) async-start(bf16[32,2,7424]{2,1,0:T(2,128)(2,1)} %copy.21), calls=%async_computation | async-start | bytes 1900544 | tf_op jit(solution)/shard_map/all_to_all | solution.py:297
  138.4 63.7 %collective-permute-start.1 = (bf16[3,464,256]{2,1,0:T(8,128)(2,1)}, bf16[3,464,256]{2,1,0:T(8,128)(2,1)S(1)}, u32[]{:S(2)}, u32[]{:S(2)}) collective-permute-start(bf16[3,464,256]{2,1,0:T(8,128)(2,1)} %get-tuple-element.10), channel_id=1, source_target_pairs={{0,1},{1,2},{2,3},{3,4},{4,5},{5,6},{6,7},{7,0},{8,9},{9,10},{10,1... | collective-permute-start | bytes 2138120 | tf_op jit(solution)/shard_map/ppermute | solution.py:259
Sparse Core Ops, SparseCore 0:
  102.0 70.2 all-gather.4
  174.2 77.8 all-gather.6

commit v2 on v0

v2 whole, which is shorter than its diff:
```python
import functools

import jax
import jax.numpy as jnp
from jax import lax
from jax.experimental import pallas as pl
from jax.experimental.pallas import tpu as pltpu
from jax.sharding import PartitionSpec as P

MESH = pl.DeviceIdType.MESH
BF16 = jnp.bfloat16
F32 = jnp.float32
I32 = jnp.int32
TOK = 256
RB = 464
CB = 256
DM = 32 * RB
IG = DM // 8
HA = 240
PC = 29
PR = 64
SR = 32
QS, QR = 112, 128


def gelu_slope(pre):
    cdf = 0.5 * (1.0 + lax.erf(pre * 0.7071067811865476))
    pdf = jnp.exp(-0.5 * pre * pre) * 0.3989422804014327
    return cdf + pre * pdf


def adam_step(param, first, second, grad):
    moment = 0.8 * first + 0.2 * grad
    spread = 0.9 * second + 0.1 * grad * grad
    updated = param - 0.1 * (moment / (jnp.sqrt(spread) + 1e-08) + 0.1 * param)
    return (updated, moment, spread)


def rows_of(f):
    return pl.ds(pl.multiple_of(f * RB, 16), RB)


def dot_t(a, b):
    return lax.dot_general(a, b, (((1,), (1,)), ((), ())), preferred_element_type=F32)


def kernel(
    tokens, out_grad, param, first_in, second_in, sources,
    input_grad, new_state, backup, written,
    tok, tokT, w, w2, rxp, sendh, rxh, sendf, rxf, sendz, rxz, dz_own, dz_all,
    first, second, st, nst, st1, st2, gp, ngp, gp1, gp2, acc, grad, p16,
    pick, merge, offer, taken, taken2, merged, rxm,
    in_sem, ag_s, ag_r, bg_s, bg_r, rs_s, rs_r, dz_s, dz_r, pe_s, pe_r, re_s, re_r, wr_s, wr_r,
):
    f = lax.axis_index("fsdp")
    h = lax.axis_index("hst")
    z, y, c = f // 8, (f // 2) % 4, f % 2
    hi, x = h // 4, h % 4
    yr, yl, yo = (y + 1) % 4, (y + 3) % 4, (y + 2) % 4
    zk = [z, z + 1 - 2 * (z % 2), (z + 2) % 4, 3 - z]

    def idx(zz, yy, cc):
        return zz * 8 + yy * 2 + cc

    def at(zz, yy, cc):
        return {"fsdp": idx(zz, yy, cc)}

    def over(ww, xx):
        return {"hst": ww * 4 + xx}

    right, left, partner, across = at(z, yr, c), at(z, yl, c), at(z, y, 1 - c), at(z, yo, c)
    line_to = [None] + [at(zk[k], y, c) for k in (1, 2, 3)]
    opposite = over(1 - hi, x)
    xs = [over(hi, (x + i) % 4) for i in (1, 2, 3)]
    swapped = {"fsdp": 4 * h + f % 4, "hst": f // 4}
    moves = f // 4 != h

    loads = [
        pltpu.make_async_copy(a, b, in_sem.at[i])
        for i, (a, b) in enumerate(((tokens, tok), (first_in, first), (second_in, second)))
    ]
    for load in loads:
        load.start()
    w[rows_of(f), :] = param[...].astype(BF16)

    barrier = pltpu.get_barrier_semaphore()
    for peer in (right, left, across, partner, *line_to[1:], opposite, *xs):
        pl.semaphore_signal(barrier, inc=1, device_id=peer, device_id_type=MESH)

    @pl.when(moves)
    def _():
        pl.semaphore_signal(barrier, inc=1, device_id=swapped, device_id_type=MESH)
        pl.semaphore_wait(barrier, 12)

    @pl.when(jnp.logical_not(moves))
    def _():
        pl.semaphore_wait(barrier, 11)

    pending = []

    def remote(src, dst, s_sem, r_sem, to):
        return pltpu.make_async_remote_copy(
            src_ref=src, dst_ref=dst, send_sem=s_sem, recv_sem=r_sem, device_id=to, device_id_type=MESH
        )

    def send(src, dst, s_sem, r_sem, to):
        copy = remote(src, dst, s_sem, r_sem, to)
        copy.start()
        pending.append(copy)
        return copy

    class Gather:
        def __init__(self, buf, s_sem, r_sem):
            self.buf, self.s, self.r = buf, s_sem, r_sem
            self.own, self.core, self.halves, self.zs, self.sent = {}, {}, {}, {}, []

        def put(self, block, lo, n, sem, to):
            ref = self.buf.at[pl.ds(pl.multiple_of(block * RB + lo, 16), n), :]
            copy = remote(ref, ref, self.s.at[sem], self.r.at[sem], to)
            copy.start()
            self.sent.append(copy)
            return copy

        def lines(self):
            for k in (1, 2, 3):
                self.zs[k] = self.put(f, 0, RB, 32 + k, line_to[k])

        def issue(self, k):
            if k:
                self.zs[k].wait_recv()
            b = idx(zk[k], y, c)
            self.own[k] = (self.put(b, 0, RB, k * 8, right), self.put(b, 0, RB, k * 8 + 1, left))
            self.core[k, 0] = self.put(b, 0, RB, k * 8 + 4, partner)

        def forward(self, k):
            self.own[k][0].wait_recv()
            b = idx(zk[k], yl, c)
            one = self.put(b, 0, HA, k * 8 + 2, right)
            self.core[k, 1] = self.put(b, 0, RB, k * 8 + 5, partner)
            self.own[k][1].wait_recv()
            b = idx(zk[k], yr, c)
            two = self.put(b, HA, RB - HA, k * 8 + 3, left)
            self.core[k, 2] = self.put(b, 0, RB, k * 8 + 6, partner)
            self.halves[k] = (one, two)

        def last(self, k):
            self.halves[k][0].wait_recv()
            self.halves[k][1].wait_recv()
            self.core[k, 3] = self.put(idx(zk[k], yo, c), 0, RB, k * 8 + 7, partner)

        def wait_core(self, k):
            for j in range(4):
                self.core[k, j].wait_recv()

    def transpose_some(lo, hi_):
        def step(i, carry):
            cols = pl.ds(pl.multiple_of(i * 512, 512), 512)
            tokT[cols, :] = tok[:, cols].T
            return carry

        lax.fori_loop(lo, hi_, step, 0)

    class Relay:
        def __init__(self, src, dst, one, two, sem):
            self.src, self.dst, self.one, self.two = src, dst, one, two
            self.s = [re_s.at[sem + i] for i in range(7)]
            self.r = [re_r.at[sem + i] for i in range(7)]

        def to_next(self):
            return remote(self.src, self.dst, self.s[0], self.r[0], over(hi, (x + 1) % 4))

        def to_column(self, q):
            return remote(self.src.at[q], self.one, self.s[1 + q], self.r[1], over(hi, q))

        def to_far(self, src):
            return remote(src, self.two, self.s[4], self.r[4], opposite)

        def start(self):
            @pl.when(x < 3)
            def _():
                self.to_next().start()

            @pl.when(x == 3)
            def _():
                for q in range(3):
                    self.to_column(q).start()
                self.to_far(self.src.at[3]).start()

        def far(self):
            @pl.when(x < 3)
            def _():
                self.to_column(0).wait_recv()
                self.to_far(self.one).start()

        def end(self):
            self.to_far(self.one).wait_recv()

            @pl.when(x == 0)
            def _():
                self.dst[0] = self.two[...]

            for q in (1, 2, 3):
                @pl.when(x == q)
                def _(q=q):
                    remote(self.two, self.dst.at[q], self.s[5], self.end_sem(q), over(hi, 0)).start()

        def end_sem(self, q):
            return (self.r[5], self.r[6], self.r[2])[q - 1]

        def arrived(self):
            @pl.when(x > 0)
            def _():
                self.to_next().wait_recv()

            @pl.when(x == 0)
            def _():
                for q in (1, 2, 3):
                    remote(self.two, self.dst.at[q], self.s[5], self.end_sem(q), over(hi, 1)).wait_recv()

        def finish(self):
            @pl.when(x < 3)
            def _():
                self.to_next().wait_send()
                self.to_far(self.one).wait_send()

            @pl.when(x == 3)
            def _():
                for q in range(3):
                    self.to_column(q).wait_send()
                self.to_far(self.src.at[3]).wait_send()

            @pl.when(x > 0)
            def _():
                remote(self.two, self.dst.at[1], self.s[5], self.r[5], over(hi, 0)).wait_send()

    slab = Gather(w, ag_s, ag_r)
    rows2 = Gather(w2, bg_s, bg_r)
    states = Relay(st, nst, st1, st2, 0)
    grads = Relay(gp, ngp, gp1, gp2, 8)

    slab.issue(0)
    slab.lines()

    row_p = lax.broadcasted_iota(I32, (PR, RB), 0)
    col_p = lax.broadcasted_iota(I32, (PR, RB), 1)
    gap0 = jnp.where(row_p < PC, col_p - row_p, -4096)
    gap1 = jnp.where((row_p >= PC) & (row_p < 2 * PC), col_p - row_p + PC, -4096)

    def pick_step(n, carry):
        writer = ((n // 2) % 4) * 8 + (n // 8) * 2 + n % 2
        a = jnp.int32(-1)
        b = jnp.int32(-1)
        for j in range(8):
            s = sources[0, writer, j]
            here = (s >= 0) & (lax.shift_right_arithmetic(s, 4) == f)
            piece = jnp.bitwise_and(s, 15)
            b = jnp.where(here & (a >= 0), piece, b)
            a = jnp.where(here & (a < 0), piece, a)
        pick[n] = ((gap0 == a * PC) | (gap1 == b * PC)).astype(F32).astype(BF16)
        return carry

    row_m = lax.broadcasted_iota(I32, (SR, 4 * PR), 0)
    col_m = lax.broadcasted_iota(I32, (SR, 4 * PR), 1)
    gap_m = jnp.where(row_m < PC, col_m - row_m, -4096)

    def merge_step(zz, carry):
        writer = idx(zz, y, c)
        entry = [sources[0, writer, j] for j in range(8)]
        owner = [lax.shift_right_arithmetic(s, 4) for s in entry]
        for j in range(8):
            rank = jnp.int32(0)
            for i in range(j):
                rank = rank + jnp.where(owner[i] == owner[j], 1, 0)
            good = (entry[j] >= 0) & (lax.shift_right_arithmetic(owner[j], 3) == z)
            start = jnp.bitwise_and(lax.shift_right_arithmetic(owner[j], 1), 3) * PR + rank * PC
            same = jnp.bitwise_and(owner[j], 1) == c
            t0 = jnp.where(good & same, start, -2048)
            t1 = jnp.where(good & jnp.logical_not(same), start, -2048)
            merge[zz, 0, pl.ds(j * SR, SR), :] = (gap_m == t0).astype(F32).astype(BF16)
            merge[zz, 1, pl.ds(j * SR, SR), :] = (gap_m == t1).astype(F32).astype(BF16)
        return carry

    lax.fori_loop(0, 16, pick_step, 0)
    loads[0].wait()
    transpose_some(0, 6)
    slab.issue(1)
    slab.forward(0)
    lax.fori_loop(16, 32, pick_step, 0)
    lax.fori_loop(0, 4, merge_step, 0)
    transpose_some(6, 12)
    slab.issue(2)
    slab.last(0)
    slab.forward(1)

    def swap_copy():
        return remote(w.at[rows_of(f), :], w2.at[rows_of(4 * h + f % 4), :], pe_s, pe_r, swapped)

    @pl.when(moves)
    def _():
        swap_copy().start()

    @pl.when(jnp.logical_not(moves))
    def _():
        w2[rows_of(f), :] = w[rows_of(f), :]

    transpose_some(12, 20)
    slab.issue(3)
    loads[1].wait()
    loads[2].wait()
    for q in range(4):
        part = pl.ds(q * QS, QR)
        st[q, 0] = param[part, :].astype(BF16)
        st[q, 1] = first[part, :].astype(BF16)
        st[q, 2] = second[part, :].astype(BF16)
    states.start()
    slab.last(1)
    slab.forward(2)
    transpose_some(20, 29)
    slab.last(2)
    slab.forward(3)

    slab.last(3)

    @pl.when(moves)
    def _():
        swap_copy().wait_recv()

    rows2.lines()
    rows2.issue(0)
    for k in range(4):
        slab.wait_core(k)

    def pre_all(k, acc_):
        cols = pl.ds(pl.multiple_of(k * 8 * RB, 128), 8 * RB)
        return acc_ + jnp.dot(tok[:, cols], w[cols, :], preferred_element_type=F32)

    pre = lax.fori_loop(0, 4, pre_all, jnp.zeros((TOK, CB), F32))
    dz_own[...] = (out_grad[...].astype(F32) * gelu_slope(pre)).astype(BF16)

    for copy in slab.sent:
        copy.wait_send()

    @pl.when(moves)
    def _():
        swap_copy().wait_send()

    swap = []
    for s, k in enumerate((3, 2, 1, 0)):
        def partner_block(j, carry, k=k, s=s):
            w[rows_of(s * 4 + j), :] = jnp.dot(
                tokT[rows_of(idx(zk[k], j, 1 - c)), :], dz_own[...], preferred_element_type=F32
            ).astype(BF16)
            return carry

        lax.fori_loop(0, 4, partner_block, 0)
        area = pl.ds(s * 4 * RB, 4 * RB)
        swap.append(send(w.at[area, :], rxp.at[area, :], rs_s.at[s], rs_r.at[s], partner))
    dz_far = send(dz_own, dz_all.at[h], dz_s.at[0], dz_r.at[0], opposite)
    dz_all[h] = dz_own[...]

    def chip_block(k, s, yy):
        mine = jnp.dot(tokT[rows_of(idx(zk[k], yy, c)), :], dz_own[...], preferred_element_type=F32)
        return mine + rxp[rows_of(s * 4 + yy), :].astype(F32)

    hsend = []
    for s, k in enumerate((3, 2, 1, 0)):
        swap[s].wait_recv()
        sendh[s] = chip_block(k, s, yo).astype(BF16)
        one = send(sendh.at[s, pl.ds(0, HA)], rxh.at[s, pl.ds(0, HA)], rs_s.at[4 + s], rs_r.at[4 + s], right)
        two = send(
            sendh.at[s, pl.ds(HA, RB - HA)], rxh.at[s, pl.ds(HA, RB - HA)], rs_s.at[8 + s], rs_r.at[8 + s], left
        )
        hsend.append((one, two))

    states.far()
    fsend = []
    zout = []

    def full(s, k):
        mine = chip_block(k, s, yr)
        hsend[s][0].wait_recv()
        sendf[s, 0, pl.ds(0, HA)] = (mine[:HA] + rxh[s, pl.ds(0, HA)].astype(F32)).astype(BF16)
        sendf[s, 0, pl.ds(HA, RB - HA)] = mine[HA:].astype(BF16)
        one = send(sendf.at[s, 0], rxf.at[s, 0], rs_s.at[12 + s], rs_r.at[12 + s], right)
        mine = chip_block(k, s, yl)
        hsend[s][1].wait_recv()
        sendf[s, 1, pl.ds(0, HA)] = mine[:HA].astype(BF16)
        sendf[s, 1, pl.ds(HA, RB - HA)] = (mine[HA:] + rxh[s, pl.ds(HA, RB - HA)].astype(F32)).astype(BF16)
        two = send(sendf.at[s, 1], rxf.at[s, 1], rs_s.at[16 + s], rs_r.at[16 + s], left)
        fsend.append((one, two))

    def ring_sum(s, k):
        mine = chip_block(k, s, y)
        fsend[s][0].wait_recv()
        fsend[s][1].wait_recv()
        return mine + rxf[s, 0].astype(F32) + rxf[s, 1].astype(F32)

    def line(s, k):
        sendz[s] = ring_sum(s, k).astype(BF16)
        zout.append(send(sendz.at[s], rxz.at[s], rs_s.at[20 + s], rs_r.at[20 + s], line_to[k]))

    full(0, 3)
    full(1, 2)
    dz_far.wait_recv()
    dz_x = []
    for i, to in enumerate(xs):
        dz_x.append(send(dz_own, dz_all.at[h], dz_s.at[1 + i], dz_r.at[1 + i], to))
        other = (1 - hi) * 4 + x
        dz_x.append(send(dz_all.at[other], dz_all.at[other], dz_s.at[4 + i], dz_r.at[4 + i], to))
    line(0, 3)
    full(2, 1)
    states.end()
    line(1, 2)
    full(3, 0)
    rows2.forward(0)
    rows2.issue(1)
    line(2, 1)
    total = ring_sum(3, 0)
    for s in range(3):
        zout[s].wait_recv()
        total = total + rxz[s].astype(F32)

    grad[...] = total * (1.0 / 90.50966799187809)
    for q in range(4):
        gp[q] = grad[pl.ds(q * QS, QR), :].astype(BF16)
    grads.start()
    updated, moment, spread = adam_step(param[...], first[...], second[...], grad[...])
    new_state[0] = updated
    new_state[1] = moment
    new_state[2] = spread
    p16[...] = updated.astype(BF16)

    ysend = {}
    for k in (3, 2, 1, 0):
        zz = zk[k]

        def offer_step(yy, carry, zz=zz):
            sel = pick[pl.ds(yy * 8 + zz * 2, 2)].reshape(2 * PR, RB)
            offer[yy, zz] = jnp.dot(sel, p16[...], preferred_element_type=F32).astype(BF16)
            return carry

        lax.fori_loop(0, 4, offer_step, 0)
        taken[y, zz] = offer[y, zz]
        for i, (yy, to) in enumerate(((yr, right), (yl, left), (yo, across))):
            ysend[k, i] = send(offer.at[yy, zz], taken.at[y, zz], wr_s.at[k * 4 + i], wr_r.at[k * 4 + i], to)
    rows2.last(0)
    rows2.issue(2)
    csend = {}
    for k in (3, 2, 1, 0):
        for i in range(3):
            ysend[k, i].wait_recv()
        src = taken.at[:, zk[k], pl.ds(pl.multiple_of((1 - c) * PR, PR), PR), :]
        csend[k] = send(src, taken2.at[zk[k]], wr_s.at[k * 4 + 3], wr_r.at[k * 4 + 3], partner)
    grads.far()
    msend = {}
    for k in (3, 2, 1, 0):
        csend[k].wait_recv()
        zz = zk[k]
        mine = taken[:, zz, pl.ds(pl.multiple_of(c * PR, PR), PR), :].reshape(4 * PR, CB)
        other = taken2[zz].reshape(4 * PR, CB)
        both = jnp.dot(merge[zz, 0], mine, preferred_element_type=F32) + jnp.dot(
            merge[zz, 1], other, preferred_element_type=F32
        )
        merged[k] = both.astype(BF16)
        if k:
            msend[k] = send(merged.at[k], rxm.at[k], wr_s.at[16 + k], wr_r.at[16 + k], line_to[k])

    rows2.forward(1)
    rows2.issue(3)
    grads.end()
    for copy in dz_x:
        copy.wait_recv()

    def columns_of(k, first_one):
        rows2.wait_core(k)
        for half in range(2):
            hh = 2 * zk[k] + half
            term = dot_t(dz_all[hh], w2[pl.ds(pl.multiple_of(hh * IG, 16), IG), :])
            if first_one and half == 0:
                acc[...] = term
            else:
                acc[...] += term

    rows2.last(1)
    rows2.forward(2)
    columns_of(0, True)
    rows2.forward(3)
    rows2.last(2)
    columns_of(1, False)
    states.arrived()
    grads.arrived()
    for q in range(4):
        n = QR if q == 3 else QS
        u, m, v = adam_step(
            nst[q, 0, :n].astype(F32), nst[q, 1, :n].astype(F32), nst[q, 2, :n].astype(F32), ngp[q, :n].astype(F32)
        )
        backup[0, pl.ds(q * QS, n)] = u
        backup[1, pl.ds(q * QS, n)] = m
        backup[2, pl.ds(q * QS, n)] = v
    columns_of(2, False)
    rows2.last(3)
    columns_of(3, False)
    input_grad[...] = acc[...].astype(BF16)
    for k in (1, 2, 3):
        msend[k].wait_recv()
    for j in range(8):
        rows = pl.ds(j * SR, SR)
        piece = (merged[0, rows].astype(F32) + rxm[1, rows].astype(F32)) + (
            rxm[2, rows].astype(F32) + rxm[3, rows].astype(F32)
        )
        written[0, 0, j] = piece[:PC]
    states.finish()
    grads.finish()
    for copy in rows2.sent + pending:
        copy.wait_send()


def kernel_call(*args):
    vmem = pl.BlockSpec(memory_space=pltpu.VMEM)
    hbm = pl.BlockSpec(memory_space=pl.ANY)
    dma = pltpu.SemaphoreType.DMA
    V = pltpu.VMEM
    return pl.pallas_call(
        kernel,
        name="slab",
        out_shape=(
            jax.ShapeDtypeStruct((TOK, IG), BF16),
            jax.ShapeDtypeStruct((3, RB, CB), F32),
            jax.ShapeDtypeStruct((3, RB, CB), F32),
            jax.ShapeDtypeStruct((1, 1, 8, PC, CB), F32),
        ),
        in_specs=[hbm, vmem, vmem, hbm, hbm, pl.BlockSpec(memory_space=pltpu.SMEM)],
        out_specs=(vmem,) * 4,
        scratch_shapes=[
            V((TOK, DM), BF16), V((DM, TOK), BF16), V((DM, CB), BF16), V((DM, CB), BF16),
            V((16 * RB, CB), BF16), V((4, RB, CB), BF16), V((4, RB, CB), BF16),
            V((4, 2, RB, CB), BF16), V((4, 2, RB, CB), BF16), V((3, RB, CB), BF16), V((3, RB, CB), BF16),
            V((TOK, CB), BF16), V((8, TOK, CB), BF16),
            V((RB, CB), F32), V((RB, CB), F32),
            V((4, 3, QR, CB), BF16), V((4, 3, QR, CB), BF16), V((3, QR, CB), BF16), V((3, QR, CB), BF16),
            V((4, QR, CB), BF16), V((4, QR, CB), BF16), V((QR, CB), BF16), V((QR, CB), BF16),
            V((TOK, IG), F32), V((RB, CB), F32), V((RB, CB), BF16),
            V((32, PR, RB), BF16), V((4, 2, 8 * SR, 4 * PR), BF16),
            V((4, 4, 2 * PR, CB), BF16), V((4, 4, 2 * PR, CB), BF16), V((4, 4, PR, CB), BF16),
            V((4, 8 * SR, CB), BF16), V((4, 8 * SR, CB), BF16),
            dma((3,)), dma((36,)), dma((36,)), dma((36,)), dma((36,)), dma((24,)), dma((24,)),
            dma((7,)), dma((7,)), dma, dma, dma((16,)), dma((16,)), dma((20,)), dma((20,)),
        ],
        compiler_params=pltpu.CompilerParams(
            collective_id=0, has_side_effects=True, vmem_limit_bytes=62 * 1024 * 1024
        ),
        cost_estimate=pl.CostEstimate(
            flops=6 * TOK * DM * CB, bytes_accessed=20_000_000, transcendentals=2 * TOK * CB
        ),
    )(*args)


def on_device(tokens, out_grad, param, first, second, sources):
    return kernel_call(tokens, out_grad, param, first, second, sources)


def solution(mesh):
    return jax.shard_map(
        on_device,
        mesh=mesh,
        in_specs=(
            P("fsdp", None),
            P("fsdp", "hst"),
            P("fsdp", "hst"),
            P("fsdp", "hst"),
            P("fsdp", "hst"),
            P("hst", None, None),
        ),
        out_specs=(
            P("fsdp", "hst"),
            P(None, "fsdp", "hst"),
            P(None, "fsdp", "hst"),
            P("hst", "fsdp", None, None, None),
        ),
        check_vma=False,
    )
```

time: 476 us -> 155 us (0.33)
  waiting for transfers between devices: 404 us -> 0 us
  Pallas kernels: 0 us -> 146 us
  matrix products: 26.1 us -> 0 us
  between operations: 13.9 us -> 0.66 us
  starting transfers between devices: 11.3 us -> 0 us
  local copies, waits for them, and re-layouts: 14.4 us -> 7.52 us
  other arithmetic: 6.63 us -> 0 us
    reduce_scatter x2 -> x0, waiting for transfers between devices: 250 us -> none  [the longest x1 140 us: on_device(): lax.psum_scatter(lax.dot_general(columns, dz, (((0,), (0,)), ((), ())), p...]
    pallas_call x0 -> x1, Pallas kernels: none -> 146 us  [kernel_call(): pl.pallas_call(kernel, name='slab', out_shape=(jax.ShapeDtypeStruct((TOK,...]
    ppermute x1 -> x0, waiting for transfers between devices: 80.1 us -> none  [from_behind(): return lax.ppermute(value, axis, pairs)]
    all_gather x1 -> x0, waiting for transfers between devices: 73.9 us -> none  [on_device(): lax.all_gather(weight16, 'fsdp', axis=0, tiled=True)]
    dot_general x4 -> x0, matrix products: 26.1 us -> none  [the longest x1 8.49 us: on_device(): lax.dot_general(columns, dz, (((0,), (0,)), ((), ())), preferred_element_...]
    all_to_all x1 -> x0, starting transfers between devices: 9.64 us -> none  [on_device(): lax.all_to_all(outgoing.astype(jnp.bfloat16), 'fsdp', split_axis=0, conca...]
    unnamed x11 -> x9, local copies, waits for them, and re-layouts: 11.2 us -> 4.34 us
  transfers between devices with their start and end apart: 5 -> 0, of which waited for: 4 -> 0; matrix products, arithmetic and copies ran while one was open for 4% -> 0% of each run, Pallas kernels for 0% -> 0%
where the time goes in v2:
time: 155 us; the launch traced here: 154 us
  Pallas kernels  146 us (94%)
  local copies, waits for them, and re-layouts  7.52 us (5%)
    pallas_call x1, Pallas kernels, kernel_call(): pl.pallas_call(kernel, name='slab', out_shape=(jax.ShapeDtypeStruct((TOK,...  146 us
    unnamed x9, local copies, waits for them, and re-layouts  4.34 us
    pallas_call x2, local copies, waits for them, and re-layouts, kernel_call(): pl.pallas_call(kernel, name='slab', out_shape=(jax.ShapeDtypeStruct((TOK,...  3.18 us

profile of v2, /device:TPU:1, one launch (start us, length us, event | category | flops | bytes accessed | tf_op | source)
XLA Modules:
  0.0 154.4 jit_solution(7893345462375685491)
XLA Ops:
  0.6 1.4 copy.10.sources
  2.0 146.3 %slab.1 = (bf16[256,1856]{1,0:T(8,128)(2,1)}, f32[3,464,256]{2,1,0:T(8,128)}, f32[3,464,256]{2,1,0:T(8,128)}, f32[1,1,8,29,256]{4,3,2,1,0:T(8,128)}) custom-call(bf16[256,14848]{1,0:T(8,128)(2,1)} %tokens.1, bf16[256,256]{1,0:T(8,128)(2,1)} %out_grad.1, f32[464,256]{1,0:T(8,128)} %param.13, f32[464,256]{1,0:T(8,128)} %first_in.1, f32[464,256]{1,0:T(8,128)} %second_in.1, ...), custom_call_target="tpu_custom_call" | custom-call | flops 5838471168 | bytes 20000000 | tf_op jit(solution)/shard_map/slab/pallas_call | solution.py:523
  148.3 0.0 copy-start.2
  148.3 0.0 copy-start.1
  148.3 2.4 %copy.11 = bf16[256,1856]{0,1:T(8,128)(2,1)} copy(bf16[256,1856]{1,0:T(8,128)(2,1)} %get-tuple-element.4) | data formatting | bytes 1900544 | tf_op jit(solution)/shard_map/slab/pallas_call | solution.py:523
  150.6 0.0 copy-done.2
  150.6 0.8 copy.12
  151.5 0.0 copy-done.1
  151.5 0.0 copy-start
  151.5 1.1 copy.15
  152.6 0.8 copy-done
  153.3 1.1 copy.16
Async XLA Ops:
  148.3 2.4 %copy-start.2 = (f32[1,1,8,29,256]{4,3,2,1,0:T(8,128)S(1)}, f32[1,1,8,29,256]{4,3,2,1,0:T(8,128)}, u32[]{:S(2)}) copy-start(f32[1,1,8,29,256]{4,3,2,1,0:T(8,128)} %get-tuple-element.7) | copy-start | bytes 712708
  148.3 3.2 %copy-start.1 = (f32[3,464,256]{2,1,0:T(8,128)S(1)}, f32[3,464,256]{2,1,0:T(8,128)}, u32[]{:S(2)}) copy-start(f32[3,464,256]{2,1,0:T(8,128)} %get-tuple-element.13) | copy-start | bytes 4276228
  151.5 1.9 %copy-start = (f32[3,464,256]{2,1,0:T(8,128)S(1)}, f32[3,464,256]{2,1,0:T(8,128)}, u32[]{:S(2)}) copy-start(f32[3,464,256]{2,1,0:T(8,128)} %get-tuple-element.14) | copy-start | bytes 4276228

commit v3 on v2

--- a/solution.py
+++ b/solution.py
@@ -50,14 +50,17 @@
     tok, tokT, w, w2, rxp, sendh, rxh, sendf, rxf, sendz, rxz, dz_own, dz_all,
     first, second, st, nst, st1, st2, gp, ngp, gp1, gp2, acc, grad, p16,
     pick, merge, offer, taken, taken2, merged, rxm,
-    in_sem, ag_s, ag_r, bg_s, bg_r, rs_s, rs_r, dz_s, dz_r, pe_s, pe_r, re_s, re_r, wr_s, wr_r,
+    xc_s, xc_r, in_sem, ag_s, ag_r, bg_s, bg_r, rs_s, rs_r, dz_s, dz_r, pe_s, pe_r, re_s, re_r, wr_s, wr_r,
 ):
     f = lax.axis_index("fsdp")
     h = lax.axis_index("hst")
     z, y, c = f // 8, (f // 2) % 4, f % 2
     hi, x = h // 4, h % 4
     yr, yl, yo = (y + 1) % 4, (y + 3) % 4, (y + 2) % 4
-    zk = [z, z + 1 - 2 * (z % 2), (z + 2) % 4, 3 - z]
+    near = z + 1 - 2 * (z % 2)
+    zx = [z, near, (z + 2) % 4, 3 - z]
+    zk = [z, near, 2 - z // 2, 3 - 3 * (z // 2)]
+    inner = (z == 1) | (z == 2)
 
     def idx(zz, yy, cc):
         return zz * 8 + yy * 2 + cc
@@ -69,11 +72,14 @@
         return {"hst": ww * 4 + xx}
 
     right, left, partner, across = at(z, yr, c), at(z, yl, c), at(z, y, 1 - c), at(z, yo, c)
-    line_to = [None] + [at(zk[k], y, c) for k in (1, 2, 3)]
+    line_to = [None] + [at(zx[k], y, c) for k in (1, 2, 3)]
     opposite = over(1 - hi, x)
     xs = [over(hi, (x + i) % 4) for i in (1, 2, 3)]
     swapped = {"fsdp": 4 * h + f % 4, "hst": f // 4}
-    moves = f // 4 != h
+    member = (z // 2 + hi) % 2
+    moves = member == 1
+    stays = member == 0
+    order2 = [member * z + (1 - member) * (2 - hi), member * near + (1 - member) * (3 - 3 * hi)]
 
     loads = [
         pltpu.make_async_copy(a, b, in_sem.at[i])
@@ -92,7 +98,7 @@
         pl.semaphore_signal(barrier, inc=1, device_id=swapped, device_id_type=MESH)
         pl.semaphore_wait(barrier, 12)
 
-    @pl.when(jnp.logical_not(moves))
+    @pl.when(stays)
     def _():
         pl.semaphore_wait(barrier, 11)
 
@@ -110,35 +116,51 @@
         return copy
 
     class Gather:
-        def __init__(self, buf, s_sem, r_sem):
-            self.buf, self.s, self.r = buf, s_sem, r_sem
-            self.own, self.core, self.halves, self.zs, self.sent = {}, {}, {}, {}, []
+        def __init__(self, buf, s_sem, r_sem, order):
+            self.buf, self.s, self.r, self.zk = buf, s_sem, r_sem, order
+            self.own, self.core, self.halves = {}, {}, {}
+            self.sent, self.some, self.came = [], [], set()
+
+        def copy(self, block, lo, n, s_sem, r_sem, to):
+            ref = self.buf.at[pl.ds(pl.multiple_of(block * RB + lo, 16), n), :]
+            return remote(ref, ref, self.s.at[s_sem], self.r.at[r_sem], to)
 
         def put(self, block, lo, n, sem, to):
-            ref = self.buf.at[pl.ds(pl.multiple_of(block * RB + lo, 16), n), :]
-            copy = remote(ref, ref, self.s.at[sem], self.r.at[sem], to)
+            copy = self.copy(block, lo, n, sem, sem, to)
             copy.start()
             self.sent.append(copy)
             return copy
 
+        def put_some(self, cond, block, s_sem, r_sem, to):
+            copy = self.copy(block, 0, RB, s_sem, r_sem, to)
+            pl.when(cond)(copy.start)
+            self.some.append((cond, copy))
+
         def lines(self):
-            for k in (1, 2, 3):
-                self.zs[k] = self.put(f, 0, RB, 32 + k, line_to[k])
+            self.put_some(z >= 0, f, 33, 33, line_to[1])
+            self.put_some(inner, f, 34, 34, line_to[3])
+
+        def arrive(self, k):
+            self.came.add(k)
+            if k == 0:
+                return
+            b = idx(self.zk[k], y, c)
+            self.copy(b, 0, RB, 33, 32 + k, line_to[1]).wait_recv()
+            self.put_some(inner, b, 34 + k, (35, 34, 35)[k - 1], (line_to[3], line_to[1], line_to[1])[k - 1])
 
         def issue(self, k):
-            if k:
-                self.zs[k].wait_recv()
-            b = idx(zk[k], y, c)
+            self.arrive(k)
+            b = idx(self.zk[k], y, c)
             self.own[k] = (self.put(b, 0, RB, k * 8, right), self.put(b, 0, RB, k * 8 + 1, left))
             self.core[k, 0] = self.put(b, 0, RB, k * 8 + 4, partner)
 
         def forward(self, k):
             self.own[k][0].wait_recv()
-            b = idx(zk[k], yl, c)
+            b = idx(self.zk[k], yl, c)
             one = self.put(b, 0, HA, k * 8 + 2, right)
             self.core[k, 1] = self.put(b, 0, RB, k * 8 + 5, partner)
             self.own[k][1].wait_recv()
-            b = idx(zk[k], yr, c)
+            b = idx(self.zk[k], yr, c)
             two = self.put(b, HA, RB - HA, k * 8 + 3, left)
             self.core[k, 2] = self.put(b, 0, RB, k * 8 + 6, partner)
             self.halves[k] = (one, two)
@@ -146,11 +168,34 @@
         def last(self, k):
             self.halves[k][0].wait_recv()
             self.halves[k][1].wait_recv()
-            self.core[k, 3] = self.put(idx(zk[k], yo, c), 0, RB, k * 8 + 7, partner)
+            self.core[k, 3] = self.put(idx(self.zk[k], yo, c), 0, RB, k * 8 + 7, partner)
 
         def wait_core(self, k):
             for j in range(4):
                 self.core[k, j].wait_recv()
+
+        def finish(self):
+            for copy in self.sent:
+                copy.wait_send()
+            for cond, copy in self.some:
+                pl.when(cond)(copy.wait_send)
+
+    class HalfGather(Gather):
+        def lines(self):
+            self.put_some(moves, f, 33, 34, line_to[1])
+            self.put_some(moves & inner, f, 34, 33, line_to[3])
+
+        def arrive(self, k):
+            self.came.add(k)
+            b = idx(self.zk[k], y, c)
+            came = self.copy(b, 0, RB, 33, 33 + k, line_to[1])
+            if k == 0:
+                pl.when(stays)(came.wait_recv)
+                self.put_some(stays & inner, b, 35, 33, line_to[1])
+            else:
+                came.wait_recv()
+                self.put_some(moves & inner, b, 36, 34, line_to[3])
+                self.put_some(stays & inner, b, 37, 34, line_to[1])
 
     def transpose_some(lo, hi_):
         def step(i, carry):
@@ -233,13 +278,13 @@
             def _():
                 remote(self.two, self.dst.at[1], self.s[5], self.r[5], over(hi, 0)).wait_send()
 
-    slab = Gather(w, ag_s, ag_r)
-    rows2 = Gather(w2, bg_s, bg_r)
+    slab = Gather(w, ag_s, ag_r, zk)
+    rows2 = HalfGather(w2, bg_s, bg_r, order2)
     states = Relay(st, nst, st1, st2, 0)
     grads = Relay(gp, ngp, gp1, gp2, 8)
 
+    slab.lines()
     slab.issue(0)
-    slab.lines()
 
     row_p = lax.broadcasted_iota(I32, (PR, RB), 0)
     col_p = lax.broadcasted_iota(I32, (PR, RB), 1)
@@ -251,7 +296,7 @@
         a = jnp.int32(-1)
         b = jnp.int32(-1)
         for j in range(8):
-            s = sources[0, writer, j]
+            s = sources[0, j, writer]
             here = (s >= 0) & (lax.shift_right_arithmetic(s, 4) == f)
             piece = jnp.bitwise_and(s, 15)
             b = jnp.where(here & (a >= 0), piece, b)
@@ -265,7 +310,7 @@
 
     def merge_step(zz, carry):
         writer = idx(zz, y, c)
-        entry = [sources[0, writer, j] for j in range(8)]
+        entry = [sources[0, j, writer] for j in range(8)]
         owner = [lax.shift_right_arithmetic(s, 4) for s in entry]
         for j in range(8):
             rank = jnp.int32(0)
@@ -284,6 +329,14 @@
     loads[0].wait()
     transpose_some(0, 6)
     slab.issue(1)
+
+    def swap_copy():
+        return remote(w.at[rows_of(f), :], w2.at[rows_of(4 * h + f % 4), :], pe_s, pe_r, swapped)
+
+    @pl.when(moves)
+    def _():
+        swap_copy().start()
+
     slab.forward(0)
     lax.fori_loop(16, 32, pick_step, 0)
     lax.fori_loop(0, 4, merge_step, 0)
@@ -291,17 +344,6 @@
     slab.issue(2)
     slab.last(0)
     slab.forward(1)
-
-    def swap_copy():
-        return remote(w.at[rows_of(f), :], w2.at[rows_of(4 * h + f % 4), :], pe_s, pe_r, swapped)
-
-    @pl.when(moves)
-    def _():
-        swap_copy().start()
-
-    @pl.when(jnp.logical_not(moves))
-    def _():
-        w2[rows_of(f), :] = w[rows_of(f), :]
 
     transpose_some(12, 20)
     slab.issue(3)
@@ -317,18 +359,32 @@
     slab.forward(2)
     transpose_some(20, 29)
     slab.last(2)
-    slab.forward(3)
-
-    slab.last(3)
 
     @pl.when(moves)
     def _():
         swap_copy().wait_recv()
 
     rows2.lines()
+    slab.forward(3)
     rows2.issue(0)
+
+    slab.last(3)
+
+    rows2.issue(1)
+
+    xcopies = {}
+    for i, to in enumerate(xs):
+        row = 4 * (4 * hi + (x + 1 + i) % 4) + c
+        for b in range(2):
+            xcopies[i, b] = send(
+                w.at[rows_of(row + 2 * b), :], w2.at[rows_of(4 * h + 2 * b + c), :],
+                xc_s.at[2 * i + b], xc_r.at[2 * i + b], to,
+            )
     for k in range(4):
         slab.wait_core(k)
+    span = pl.ds(pl.multiple_of(h * IG, 16), IG)
+    own_rows = pltpu.make_async_copy(w.at[span, :], w2.at[span, :], in_sem.at[3])
+    own_rows.start()
 
     def pre_all(k, acc_):
         cols = pl.ds(pl.multiple_of(k * 8 * RB, 128), 8 * RB)
@@ -337,8 +393,7 @@
     pre = lax.fori_loop(0, 4, pre_all, jnp.zeros((TOK, CB), F32))
     dz_own[...] = (out_grad[...].astype(F32) * gelu_slope(pre)).astype(BF16)
 
-    for copy in slab.sent:
-        copy.wait_send()
+    slab.finish()
 
     @pl.when(moves)
     def _():
@@ -347,23 +402,25 @@
     swap = []
     for s, k in enumerate((3, 2, 1, 0)):
         def partner_block(j, carry, k=k, s=s):
-            w[rows_of(s * 4 + j), :] = jnp.dot(
-                tokT[rows_of(idx(zk[k], j, 1 - c)), :], dz_own[...], preferred_element_type=F32
+            w[rows_of(16 * (1 - hi) + s * 4 + j), :] = jnp.dot(
+                tokT[rows_of(idx(zx[k], j, 1 - c)), :], dz_own[...], preferred_element_type=F32
             ).astype(BF16)
             return carry
 
         lax.fori_loop(0, 4, partner_block, 0)
         area = pl.ds(s * 4 * RB, 4 * RB)
-        swap.append(send(w.at[area, :], rxp.at[area, :], rs_s.at[s], rs_r.at[s], partner))
+        part = pl.ds(pl.multiple_of((16 * (1 - hi) + s * 4) * RB, 16), 4 * RB)
+        swap.append(send(w.at[part, :], rxp.at[area, :], rs_s.at[s], rs_r.at[s], partner))
     dz_far = send(dz_own, dz_all.at[h], dz_s.at[0], dz_r.at[0], opposite)
     dz_all[h] = dz_own[...]
 
     def chip_block(k, s, yy):
-        mine = jnp.dot(tokT[rows_of(idx(zk[k], yy, c)), :], dz_own[...], preferred_element_type=F32)
+        mine = jnp.dot(tokT[rows_of(idx(zx[k], yy, c)), :], dz_own[...], preferred_element_type=F32)
         return mine + rxp[rows_of(s * 4 + yy), :].astype(F32)
 
     hsend = []
-    for s, k in enumerate((3, 2, 1, 0)):
+
+    def half(s, k):
         swap[s].wait_recv()
         sendh[s] = chip_block(k, s, yo).astype(BF16)
         one = send(sendh.at[s, pl.ds(0, HA)], rxh.at[s, pl.ds(0, HA)], rs_s.at[4 + s], rs_r.at[4 + s], right)
@@ -372,7 +429,6 @@
         )
         hsend.append((one, two))
 
-    states.far()
     fsend = []
     zout = []
 
@@ -399,21 +455,25 @@
         sendz[s] = ring_sum(s, k).astype(BF16)
         zout.append(send(sendz.at[s], rxz.at[s], rs_s.at[20 + s], rs_r.at[20 + s], line_to[k]))
 
+    half(0, 3)
+    half(1, 2)
     full(0, 3)
-    full(1, 2)
+    half(2, 1)
     dz_far.wait_recv()
     dz_x = []
     for i, to in enumerate(xs):
         dz_x.append(send(dz_own, dz_all.at[h], dz_s.at[1 + i], dz_r.at[1 + i], to))
         other = (1 - hi) * 4 + x
         dz_x.append(send(dz_all.at[other], dz_all.at[other], dz_s.at[4 + i], dz_r.at[4 + i], to))
+    full(1, 2)
+    states.far()
     line(0, 3)
+    half(3, 0)
     full(2, 1)
-    states.end()
     line(1, 2)
     full(3, 0)
     rows2.forward(0)
-    rows2.issue(1)
+    states.end()
     line(2, 1)
     total = ring_sum(3, 0)
     for s in range(3):
@@ -432,7 +492,7 @@
 
     ysend = {}
     for k in (3, 2, 1, 0):
-        zz = zk[k]
+        zz = zx[k]
 
         def offer_step(yy, carry, zz=zz):
             sel = pick[pl.ds(yy * 8 + zz * 2, 2)].reshape(2 * PR, RB)
@@ -443,19 +503,24 @@
         taken[y, zz] = offer[y, zz]
         for i, (yy, to) in enumerate(((yr, right), (yl, left), (yo, across))):
             ysend[k, i] = send(offer.at[yy, zz], taken.at[y, zz], wr_s.at[k * 4 + i], wr_r.at[k * 4 + i], to)
-    rows2.last(0)
-    rows2.issue(2)
+    rows2.forward(1)
+    xcore = {}
+    for i in range(3):
+        for b in range(2):
+            xcopies[i, b].wait_recv()
+            slot = rows_of(4 * (4 * hi + (x + 3 - i) % 4) + 2 * b + c)
+            xcore[i, b] = send(w2.at[slot, :], w2.at[slot, :], xc_s.at[6 + 2 * i + b], xc_r.at[6 + 2 * i + b], partner)
     csend = {}
     for k in (3, 2, 1, 0):
         for i in range(3):
             ysend[k, i].wait_recv()
-        src = taken.at[:, zk[k], pl.ds(pl.multiple_of((1 - c) * PR, PR), PR), :]
-        csend[k] = send(src, taken2.at[zk[k]], wr_s.at[k * 4 + 3], wr_r.at[k * 4 + 3], partner)
+        src = taken.at[:, zx[k], pl.ds(pl.multiple_of((1 - c) * PR, PR), PR), :]
+        csend[k] = send(src, taken2.at[zx[k]], wr_s.at[k * 4 + 3], wr_r.at[k * 4 + 3], partner)
     grads.far()
     msend = {}
     for k in (3, 2, 1, 0):
         csend[k].wait_recv()
-        zz = zk[k]
+        zz = zx[k]
         mine = taken[:, zz, pl.ds(pl.multiple_of(c * PR, PR), PR), :].reshape(4 * PR, CB)
         other = taken2[zz].reshape(4 * PR, CB)
         both = jnp.dot(merge[zz, 0], mine, preferred_element_type=F32) + jnp.dot(
@@ -465,28 +530,25 @@
         if k:
             msend[k] = send(merged.at[k], rxm.at[k], wr_s.at[16 + k], wr_r.at[16 + k], line_to[k])
 
-    rows2.forward(1)
-    rows2.issue(3)
+    rows2.last(0)
     grads.end()
     for copy in dz_x:
         copy.wait_recv()
-
-    def columns_of(k, first_one):
-        rows2.wait_core(k)
-        for half in range(2):
-            hh = 2 * zk[k] + half
-            term = dot_t(dz_all[hh], w2[pl.ds(pl.multiple_of(hh * IG, 16), IG), :])
-            if first_one and half == 0:
-                acc[...] = term
-            else:
-                acc[...] += term
-
+    own_rows.wait()
+
+    def add_term(hh, first_one=False):
+        term = dot_t(w2[pl.ds(pl.multiple_of(hh * IG, 16), IG), :], dz_all[hh])
+        if first_one:
+            acc[...] = term
+        else:
+            acc[...] += term
+
+    add_term(h, True)
     rows2.last(1)
-    rows2.forward(2)
-    columns_of(0, True)
-    rows2.forward(3)
-    rows2.last(2)
-    columns_of(1, False)
+    for i in range(3):
+        for b in range(2):
+            xcore[i, b].wait_recv()
+        add_term(4 * hi + (x + 3 - i) % 4)
     states.arrived()
     grads.arrived()
     for q in range(4):
@@ -497,9 +559,10 @@
         backup[0, pl.ds(q * QS, n)] = u
         backup[1, pl.ds(q * QS, n)] = m
         backup[2, pl.ds(q * QS, n)] = v
-    columns_of(2, False)
-    rows2.last(3)
-    columns_of(3, False)
+    for k in range(2):
+        rows2.wait_core(k)
+        for half_ in range(2):
+            add_term(2 * order2[k] + half_)
     input_grad[...] = acc[...].astype(BF16)
     for k in (1, 2, 3):
         msend[k].wait_recv()
@@ -508,10 +571,11 @@
         piece = (merged[0, rows].astype(F32) + rxm[1, rows].astype(F32)) + (
             rxm[2, rows].astype(F32) + rxm[3, rows].astype(F32)
         )
-        written[0, 0, j] = piece[:PC]
+        written[0, 0, :, j, :] = piece[:PC]
     states.finish()
     grads.finish()
-    for copy in rows2.sent + pending:
+    rows2.finish()
+    for copy in pending:
         copy.wait_send()
 
 
@@ -524,10 +588,10 @@
         kernel,
         name="slab",
         out_shape=(
-            jax.ShapeDtypeStruct((TOK, IG), BF16),
-            jax.ShapeDtypeStruct((3, RB, CB), F32),
-            jax.ShapeDtypeStruct((3, RB, CB), F32),
-            jax.ShapeDtypeStruct((1, 1, 8, PC, CB), F32),
+            pltpu.VMEM((IG, TOK), BF16),
+            pltpu.VMEM((3, RB, CB), F32),
+            pltpu.VMEM((3, RB, CB), F32),
+            pltpu.VMEM((1, 1, PC, 8, CB), F32),
         ),
         in_specs=[hbm, vmem, vmem, hbm, hbm, pl.BlockSpec(memory_space=pltpu.SMEM)],
         out_specs=(vmem,) * 4,
@@ -539,15 +603,15 @@
             V((RB, CB), F32), V((RB, CB), F32),
             V((4, 3, QR, CB), BF16), V((4, 3, QR, CB), BF16), V((3, QR, CB), BF16), V((3, QR, CB), BF16),
             V((4, QR, CB), BF16), V((4, QR, CB), BF16), V((QR, CB), BF16), V((QR, CB), BF16),
-            V((TOK, IG), F32), V((RB, CB), F32), V((RB, CB), BF16),
+            V((IG, TOK), F32), V((RB, CB), F32), V((RB, CB), BF16),
             V((32, PR, RB), BF16), V((4, 2, 8 * SR, 4 * PR), BF16),
             V((4, 4, 2 * PR, CB), BF16), V((4, 4, 2 * PR, CB), BF16), V((4, 4, PR, CB), BF16),
             V((4, 8 * SR, CB), BF16), V((4, 8 * SR, CB), BF16),
-            dma((3,)), dma((36,)), dma((36,)), dma((36,)), dma((36,)), dma((24,)), dma((24,)),
+            dma((12,)), dma((12,)), dma((8,)), dma((38,)), dma((38,)), dma((38,)), dma((38,)), dma((24,)), dma((24,)),
             dma((7,)), dma((7,)), dma, dma, dma((16,)), dma((16,)), dma((20,)), dma((20,)),
         ],
         compiler_params=pltpu.CompilerParams(
-            collective_id=0, has_side_effects=True, vmem_limit_bytes=62 * 1024 * 1024
+            collective_id=0, has_side_effects=True, vmem_limit_bytes=58 * 1024 * 1024
         ),
         cost_estimate=pl.CostEstimate(
             flops=6 * TOK * DM * CB, bytes_accessed=20_000_000, transcendentals=2 * TOK * CB
@@ -556,7 +620,10 @@
 
 
 def on_device(tokens, out_grad, param, first, second, sources):
-    return kernel_call(tokens, out_grad, param, first, second, sources)
+    input_grad, new_state, backup, written = kernel_call(
+        tokens, out_grad, param, first, second, sources.transpose(0, 2, 1)
+    )
+    return (input_grad.T, new_state, backup, written.transpose(0, 1, 3, 2, 4))
 
 
 def solution(mesh):

time: 155 us -> 146 us (0.942)
  Pallas kernels: 146 us -> 142 us
  local copies, waits for them, and re-layouts: 7.52 us -> 3.81 us
    pallas_call x1, Pallas kernels: 146 us -> 142 us  [kernel_call(): pl.pallas_call(kernel, name='slab', out_shape=(pltpu.VMEM((IG, TOK), BF16...]
    pallas_call x2 -> x0, local copies, waits for them, and re-layouts: 3.18 us -> none  [kernel_call(): pl.pallas_call(kernel, name='slab', out_shape=(jax.ShapeDtypeStruct((TOK,...]
    unnamed x9 -> x4, local copies, waits for them, and re-layouts: 4.34 us -> 3.81 us
where the time goes in v3:
time: 146 us
  Pallas kernels  142 us (97%)
  local copies, waits for them, and re-layouts  3.81 us (3%)
    pallas_call x1, Pallas kernels, kernel_call(): pl.pallas_call(kernel, name='slab', out_shape=(pltpu.VMEM((IG, TOK), BF16...  142 us
    unnamed x4, local copies, waits for them, and re-layouts  3.81 us

profile of v3, /device:TPU:1, one launch (start us, length us, event | category | flops | bytes accessed | tf_op | source)
XLA Modules:
  0.0 146.0 jit_solution(12776250904626270447)
XLA Ops:
  0.6 141.5 %slab.1 = (bf16[1856,256]{1,0:T(8,128)(2,1)S(1)}, f32[3,464,256]{2,1,0:T(8,128)S(1)}, f32[3,464,256]{2,1,0:T(8,128)S(1)}, f32[1,1,29,8,256]{4,3,2,1,0:T(8,128)S(1)}) custom-call(bf16[256,14848]{1,0:T(8,128)(2,1)} %tokens.1, bf16[256,256]{1,0:T(8,128)(2,1)} %out_grad.1, f32[464,256]{1,0:T(8,128)} %param.13, f32[464,256]{1,0:T(8,128)} %first_in.1, ...), custom_call_target="tpu_custom_call" | custom-call | flops 5838471168 | bytes 20000000 | tf_op jit(solution)/shard_map/slab/pallas_call | solution.py:587
  142.1 0.9 copy.14
  143.1 0.7 copy.17
  143.8 1.1 copy.15
  144.9 1.1 copy.16

commit v4 on v3

--- a/solution.py
+++ b/solution.py
@@ -87,7 +87,6 @@
     ]
     for load in loads:
         load.start()
-    w[rows_of(f), :] = param[...].astype(BF16)
 
     barrier = pltpu.get_barrier_semaphore()
     for peer in (right, left, across, partner, *line_to[1:], opposite, *xs):
@@ -96,6 +95,11 @@
     @pl.when(moves)
     def _():
         pl.semaphore_signal(barrier, inc=1, device_id=swapped, device_id_type=MESH)
+
+    w[rows_of(f), :] = param[...].astype(BF16)
+
+    @pl.when(moves)
+    def _():
         pl.semaphore_wait(barrier, 12)
 
     @pl.when(stays)
@@ -354,20 +358,32 @@
         st[q, 0] = param[part, :].astype(BF16)
         st[q, 1] = first[part, :].astype(BF16)
         st[q, 2] = second[part, :].astype(BF16)
-    states.start()
+
+    @pl.when(moves)
+    def _():
+        swap_copy().wait_recv()
+
+    rows2.lines()
     slab.last(1)
     slab.forward(2)
     transpose_some(20, 29)
     slab.last(2)
 
-    @pl.when(moves)
-    def _():
-        swap_copy().wait_recv()
-
-    rows2.lines()
     slab.forward(3)
     rows2.issue(0)
 
+
+    def add_pre(k):
+        part = pl.ds(pl.multiple_of(zk[k] * 8 * RB, 128), 8 * RB)
+        term = jnp.dot(tok[:, part], w[part, :], preferred_element_type=F32)
+        if k:
+            acc[pl.ds(0, TOK), :] += term
+        else:
+            acc[pl.ds(0, TOK), :] = term
+
+    for k in range(2):
+        slab.wait_core(k)
+        add_pre(k)
     slab.last(3)
 
     rows2.issue(1)
@@ -380,17 +396,15 @@
                 w.at[rows_of(row + 2 * b), :], w2.at[rows_of(4 * h + 2 * b + c), :],
                 xc_s.at[2 * i + b], xc_r.at[2 * i + b], to,
             )
-    for k in range(4):
+    for k in range(2, 4):
         slab.wait_core(k)
     span = pl.ds(pl.multiple_of(h * IG, 16), IG)
     own_rows = pltpu.make_async_copy(w.at[span, :], w2.at[span, :], in_sem.at[3])
     own_rows.start()
 
-    def pre_all(k, acc_):
-        cols = pl.ds(pl.multiple_of(k * 8 * RB, 128), 8 * RB)
-        return acc_ + jnp.dot(tok[:, cols], w[cols, :], preferred_element_type=F32)
-
-    pre = lax.fori_loop(0, 4, pre_all, jnp.zeros((TOK, CB), F32))
+    for k in (2, 3):
+        add_pre(k)
+    pre = acc[pl.ds(0, TOK), :]
     dz_own[...] = (out_grad[...].astype(F32) * gelu_slope(pre)).astype(BF16)
 
     slab.finish()
@@ -411,6 +425,7 @@
         area = pl.ds(s * 4 * RB, 4 * RB)
         part = pl.ds(pl.multiple_of((16 * (1 - hi) + s * 4) * RB, 16), 4 * RB)
         swap.append(send(w.at[part, :], rxp.at[area, :], rs_s.at[s], rs_r.at[s], partner))
+    states.start()
     dz_far = send(dz_own, dz_all.at[h], dz_s.at[0], dz_r.at[0], opposite)
     dz_all[h] = dz_own[...]
 
@@ -466,14 +481,12 @@
         other = (1 - hi) * 4 + x
         dz_x.append(send(dz_all.at[other], dz_all.at[other], dz_s.at[4 + i], dz_r.at[4 + i], to))
     full(1, 2)
-    states.far()
     line(0, 3)
     half(3, 0)
     full(2, 1)
     line(1, 2)
+    states.far()
     full(3, 0)
-    rows2.forward(0)
-    states.end()
     line(2, 1)
     total = ring_sum(3, 0)
     for s in range(3):
@@ -490,35 +503,31 @@
     new_state[2] = spread
     p16[...] = updated.astype(BF16)
 
-    ysend = {}
-    for k in (3, 2, 1, 0):
+    ysend, csend, msend, xcore = {}, {}, {}, {}
+
+    def offer_to(k):
         zz = zx[k]
 
-        def offer_step(yy, carry, zz=zz):
+        def offer_step(yy, carry):
             sel = pick[pl.ds(yy * 8 + zz * 2, 2)].reshape(2 * PR, RB)
             offer[yy, zz] = jnp.dot(sel, p16[...], preferred_element_type=F32).astype(BF16)
             return carry
 
         lax.fori_loop(0, 4, offer_step, 0)
+
+    def offer_send(k):
+        zz = zx[k]
+        for i, (yy, to) in enumerate(((yo, across), (yr, right), (yl, left))):
+            ysend[k, i] = send(offer.at[yy, zz], taken.at[y, zz], wr_s.at[k * 4 + i], wr_r.at[k * 4 + i], to)
         taken[y, zz] = offer[y, zz]
-        for i, (yy, to) in enumerate(((yr, right), (yl, left), (yo, across))):
-            ysend[k, i] = send(offer.at[yy, zz], taken.at[y, zz], wr_s.at[k * 4 + i], wr_r.at[k * 4 + i], to)
-    rows2.forward(1)
-    xcore = {}
-    for i in range(3):
-        for b in range(2):
-            xcopies[i, b].wait_recv()
-            slot = rows_of(4 * (4 * hi + (x + 3 - i) % 4) + 2 * b + c)
-            xcore[i, b] = send(w2.at[slot, :], w2.at[slot, :], xc_s.at[6 + 2 * i + b], xc_r.at[6 + 2 * i + b], partner)
-    csend = {}
-    for k in (3, 2, 1, 0):
+
+    def to_core(k):
         for i in range(3):
             ysend[k, i].wait_recv()
         src = taken.at[:, zx[k], pl.ds(pl.multiple_of((1 - c) * PR, PR), PR), :]
         csend[k] = send(src, taken2.at[zx[k]], wr_s.at[k * 4 + 3], wr_r.at[k * 4 + 3], partner)
-    grads.far()
-    msend = {}
-    for k in (3, 2, 1, 0):
+
+    def merge_to(k):
         csend[k].wait_recv()
         zz = zx[k]
         mine = taken[:, zz, pl.ds(pl.multiple_of(c * PR, PR), PR), :].reshape(4 * PR, CB)
@@ -529,6 +538,35 @@
         merged[k] = both.astype(BF16)
         if k:
             msend[k] = send(merged.at[k], rxm.at[k], wr_s.at[16 + k], wr_r.at[16 + k], line_to[k])
+
+    def x_to_core(i):
+        for b in range(2):
+            xcopies[i, b].wait_recv()
+            slot = rows_of(4 * (4 * hi + (x + 3 - i) % 4) + 2 * b + c)
+            xcore[i, b] = send(w2.at[slot, :], w2.at[slot, :], xc_s.at[6 + 2 * i + b], xc_r.at[6 + 2 * i + b], partner)
+
+    offer_to(3)
+    offer_send(3)
+    offer_to(2)
+    offer_send(2)
+    offer_to(1)
+    offer_to(0)
+    rows2.forward(0)
+    to_core(3)
+    offer_send(1)
+    to_core(2)
+    offer_send(0)
+    rows2.forward(1)
+    merge_to(3)
+    merge_to(2)
+    states.end()
+    grads.far()
+    for i in range(3):
+        x_to_core(i)
+    to_core(1)
+    to_core(0)
+    merge_to(1)
+    merge_to(0)
 
     rows2.last(0)
     grads.end()

time: 146 us -> 142 us (0.973)
  Pallas kernels: 142 us -> 137 us
    pallas_call x1, Pallas kernels: 142 us -> 137 us  [kernel_call(): pl.pallas_call(kernel, name='slab', out_shape=(pltpu.VMEM((IG, TOK), BF16...]
where the time goes in v4:
time: 142 us
  Pallas kernels  137 us (96%)
  local copies, waits for them, and re-layouts  3.81 us (3%)
    pallas_call x1, Pallas kernels, kernel_call(): pl.pallas_call(kernel, name='slab', out_shape=(pltpu.VMEM((IG, TOK), BF16...  137 us
    unnamed x4, local copies, waits for them, and re-layouts  3.81 us

profile of v4, /device:TPU:1, one launch (start us, length us, event | category | flops | bytes accessed | tf_op | source)
XLA Modules:
  0.0 141.8 jit_solution(8309429015054272810)
XLA Ops:
  0.6 137.4 %slab.1 = (bf16[1856,256]{1,0:T(8,128)(2,1)S(1)}, f32[3,464,256]{2,1,0:T(8,128)S(1)}, f32[3,464,256]{2,1,0:T(8,128)S(1)}, f32[1,1,29,8,256]{4,3,2,1,0:T(8,128)S(1)}) custom-call(bf16[256,14848]{1,0:T(8,128)(2,1)} %tokens.1, bf16[256,256]{1,0:T(8,128)(2,1)} %out_grad.1, f32[464,256]{1,0:T(8,128)} %param.13, f32[464,256]{1,0:T(8,128)} %first_in.1, ...), custom_call_target="tpu_custom_call" | custom-call | flops 5838471168 | bytes 20000000 | tf_op jit(solution)/shard_map/slab/pallas_call | solution.py:625
  138.0 0.9 copy.14
  139.0 0.7 copy.17
  139.6 1.1 copy.15
  140.7 1.1 copy.16

commit v5 on v4

--- a/solution.py
+++ b/solution.py
@@ -370,7 +370,6 @@
     slab.last(2)
 
     slab.forward(3)
-    rows2.issue(0)
 
 
     def add_pre(k):
@@ -384,10 +383,43 @@
     for k in range(2):
         slab.wait_core(k)
         add_pre(k)
+    rows2.issue(0)
+    rows2.issue(1)
     slab.last(3)
 
-    rows2.issue(1)
-
+
+    for k in range(2, 4):
+        slab.wait_core(k)
+    span = pl.ds(pl.multiple_of(h * IG, 16), IG)
+    own_rows = pltpu.make_async_copy(w.at[span, :], w2.at[span, :], in_sem.at[3])
+    own_rows.start()
+
+    for k in (2, 3):
+        add_pre(k)
+    pre = acc[pl.ds(0, TOK), :]
+    dz_own[...] = (out_grad[...].astype(F32) * gelu_slope(pre)).astype(BF16)
+
+    slab.finish()
+
+    @pl.when(moves)
+    def _():
+        swap_copy().wait_send()
+
+    swap = []
+    for s, k in enumerate((3, 2, 1, 0)):
+        def partner_block(j, carry, k=k, s=s):
+            w[rows_of(16 * (1 - hi) + s * 4 + j), :] = jnp.dot(
+                tokT[rows_of(idx(zx[k], j, 1 - c)), :], dz_own[...], preferred_element_type=F32
+            ).astype(BF16)
+            return carry
+
+        lax.fori_loop(0, 4, partner_block, 0)
+        area = pl.ds(s * 4 * RB, 4 * RB)
+        part = pl.ds(pl.multiple_of((16 * (1 - hi) + s * 4) * RB, 16), 4 * RB)
+        swap.append(send(w.at[part, :], rxp.at[area, :], rs_s.at[s], rs_r.at[s], partner))
+    dz_far = send(dz_own, dz_all.at[h], dz_s.at[0], dz_r.at[0], opposite)
+    dz_all[h] = dz_own[...]
+    states.start()
     xcopies = {}
     for i, to in enumerate(xs):
         row = 4 * (4 * hi + (x + 1 + i) % 4) + c
@@ -396,38 +428,6 @@
                 w.at[rows_of(row + 2 * b), :], w2.at[rows_of(4 * h + 2 * b + c), :],
                 xc_s.at[2 * i + b], xc_r.at[2 * i + b], to,
             )
-    for k in range(2, 4):
-        slab.wait_core(k)
-    span = pl.ds(pl.multiple_of(h * IG, 16), IG)
-    own_rows = pltpu.make_async_copy(w.at[span, :], w2.at[span, :], in_sem.at[3])
-    own_rows.start()
-
-    for k in (2, 3):
-        add_pre(k)
-    pre = acc[pl.ds(0, TOK), :]
-    dz_own[...] = (out_grad[...].astype(F32) * gelu_slope(pre)).astype(BF16)
-
-    slab.finish()
-
-    @pl.when(moves)
-    def _():
-        swap_copy().wait_send()
-
-    swap = []
-    for s, k in enumerate((3, 2, 1, 0)):
-        def partner_block(j, carry, k=k, s=s):
-            w[rows_of(16 * (1 - hi) + s * 4 + j), :] = jnp.dot(
-                tokT[rows_of(idx(zx[k], j, 1 - c)), :], dz_own[...], preferred_element_type=F32
-            ).astype(BF16)
-            return carry
-
-        lax.fori_loop(0, 4, partner_block, 0)
-        area = pl.ds(s * 4 * RB, 4 * RB)
-        part = pl.ds(pl.multiple_of((16 * (1 - hi) + s * 4) * RB, 16), 4 * RB)
-        swap.append(send(w.at[part, :], rxp.at[area, :], rs_s.at[s], rs_r.at[s], partner))
-    states.start()
-    dz_far = send(dz_own, dz_all.at[h], dz_s.at[0], dz_r.at[0], opposite)
-    dz_all[h] = dz_own[...]
 
     def chip_block(k, s, yy):
         mine = jnp.dot(tokT[rows_of(idx(zx[k], yy, c)), :], dz_own[...], preferred_element_type=F32)

time: 142 us -> 140 us (0.986)
    pallas_call x1, Pallas kernels: 137 us -> 136 us  [kernel_call(): pl.pallas_call(kernel, name='slab', out_shape=(pltpu.VMEM((IG, TOK), BF16...]
where the time goes in v5:
time: 140 us
  Pallas kernels  136 us (97%)
  local copies, waits for them, and re-layouts  3.81 us (3%)
    pallas_call x1, Pallas kernels, kernel_call(): pl.pallas_call(kernel, name='slab', out_shape=(pltpu.VMEM((IG, TOK), BF16...  136 us
    unnamed x4, local copies, waits for them, and re-layouts  3.81 us

profile of v5, /device:TPU:1, one launch (start us, length us, event | category | flops | bytes accessed | tf_op | source)
XLA Modules:
  0.0 140.0 jit_solution(6622680088171651138)
XLA Ops:
  0.6 135.5 %slab.1 = (bf16[1856,256]{1,0:T(8,128)(2,1)S(1)}, f32[3,464,256]{2,1,0:T(8,128)S(1)}, f32[3,464,256]{2,1,0:T(8,128)S(1)}, f32[1,1,29,8,256]{4,3,2,1,0:T(8,128)S(1)}) custom-call(bf16[256,14848]{1,0:T(8,128)(2,1)} %tokens.1, bf16[256,256]{1,0:T(8,128)(2,1)} %out_grad.1, f32[464,256]{1,0:T(8,128)} %param.13, f32[464,256]{1,0:T(8,128)} %first_in.1, ...), custom_call_target="tpu_custom_call" | custom-call | flops 5838471168 | bytes 20000000 | tf_op jit(solution)/shard_map/slab/pallas_call | solution.py:625
  136.2 0.9 copy.14
  137.1 0.7 copy.17
  137.8 1.1 copy.15
  138.9 1.1 copy.16
